TPU v7x, 512 devices: a whole 4x8x8 slice. The times are simulated.
512 devices in a mesh: ch: 256 (over y, x_lo, z, core), seg: 2 (over x_hi).
Axes of the slice: x: 4 (x_hi: 2, x_lo: 2; x = x_hi * 2 + x_lo), y: 8, z: 8, core: 2. Of those that a mesh axis runs over, the one named last changes fastest.
Arguments:
- spectra: bfloat16 [256, 6, 2, 128, 512], P('ch', 'seg'), may hold values from -6 to 6
- plan: int32 [2, 256], P(None, 'ch'), may hold values from 0 to 255, as said below
Outputs:
- correlations: bfloat16 [256, 2, 128, 128, 128], P('ch', 'seg')
Inputs may be any that keep to these rules, and one draw needn't show every extreme that they name: For each round r there is a mask m_r, 1 to 255, with plan[r, b] = b XOR m_r for every block b; the masks of different rounds differ.
All inputs are finite; a program needn't handle non-finite values.
Results may differ from a plain program's by a relative error of at most 0.0055.
Values may be sent and summed in bfloat16 or wider, within the bound.
A program may use at most 64 MiB of HBM per device.

v0:
```python
import math

import jax
import jax.numpy as jnp
from jax import lax
from jax.sharding import PartitionSpec as P

LAGS = 128


def swapped(value, axis, bit):
    mask = 2**bit
    pairs = [(source, source ^ mask) for source in range(lax.axis_size(axis))]
    return lax.ppermute(value, axis, pairs)


def lag_table(bin_count, lag_count):
    bin_index = jnp.arange(bin_count, dtype=jnp.int32)
    lag_index = jnp.arange(lag_count, dtype=jnp.int32) - lag_count // 2
    product = lag_index[:, None] * bin_index[None, :] % (2 * bin_count)
    angles = product.astype(jnp.float32) * (jnp.pi / bin_count)
    return jnp.concatenate([jnp.cos(angles), -jnp.sin(angles)], axis=1).astype(jnp.bfloat16)


def correlate(left_spec, right_spec, table_matrix):
    channels = left_spec.shape[2]
    bin_count = left_spec.shape[3]
    lag_count = table_matrix.shape[0]
    row_block = min(channels, 16)
    right_both = jnp.concatenate([right_spec[:, 0], right_spec[:, 1]], axis=0)

    def one_slab(number, collected):
        first = number * row_block
        row_slab = lax.dynamic_slice_in_dim(left_spec, first, row_block, 2)
        plain_rows = jnp.concatenate([row_slab[:, 0], row_slab[:, 1]], axis=0)
        turned_rows = jnp.concatenate([row_slab[:, 1], -row_slab[:, 0]], axis=0)
        left_both = jnp.concatenate([plain_rows, turned_rows], axis=1)
        both_parts = jnp.einsum(
            "sif,sjf->fij", left_both, right_both, preferred_element_type=jnp.float32
        ).astype(jnp.bfloat16)
        spectrum = jnp.concatenate(
            [both_parts[:, :row_block], both_parts[:, row_block:]], axis=0
        ).reshape(2 * bin_count, row_block * channels)
        lag_part = jnp.dot(table_matrix, spectrum, preferred_element_type=jnp.float32).reshape(
            lag_count, row_block, channels
        )
        return lax.dynamic_update_slice_in_dim(collected, lag_part, first, 1)

    start_value = jnp.zeros((lag_count, channels, channels), jnp.float32)
    return lax.fori_loop(0, channels // row_block, one_slab, start_value)


def route_block(block_data, partner_mask):
    bit_count = lax.axis_size("ch").bit_length() - 1
    bit_order = list(range(bit_count))
    for bit_number in bit_order:

        def move(current, bit_number=bit_number):
            return swapped(current, "ch", bit_number)

        taken = jnp.bitwise_and(jnp.right_shift(partner_mask, bit_number), 1) == 1
        arrived = move(block_data)
        block_data = jnp.where(taken, arrived, block_data)
    return block_data


def per_device(spectra, plan):
    mine_block = spectra[0]
    seg_dev = mine_block.shape[0]
    bin_count = mine_block.shape[3]
    table_matrix = lag_table(bin_count, LAGS)
    group_count = lax.axis_size("seg")
    factor = 1.0 / math.sqrt(2.0 * seg_dev * group_count * bin_count)
    position = lax.axis_index("ch")
    all_groups = lax.all_gather(spectra, "seg", axis=1, tiled=True)[0]
    my_round = lax.axis_index("seg")
    round_entry = lax.dynamic_index_in_dim(plan[:, 0], my_round, keepdims=False)
    partner_mask = jnp.bitwise_xor(round_entry, position)
    partner_block = route_block(all_groups, partner_mask)
    lags_now = correlate(all_groups, partner_block, table_matrix)
    return (lags_now * factor).astype(jnp.bfloat16)[None, None]


def solution(mesh):
    in_specs = (P("ch", "seg", None, None, None), P(None, "ch"))
    out_specs = P("ch", "seg", None, None, None)
    return jax.shard_map(
        per_device, mesh=mesh, in_specs=in_specs, out_specs=out_specs, check_vma=False
    )
```

profile of v0, /device:TPU:6, one launch (start us, length us, event | category | flops | bytes accessed | tf_op | source)
XLA Modules:
  0.0 584.8 jit_solution(15785274758858531658)
XLA Ops:
  7.3 41.9 %all-gather.2.cloned.1.call-done = bf16[1,6,2,128,512]{4,3,2,0,1:T(8,128)(2,1)} async-done(((bf16[1,3,2,128,512]{4,3,2,0,1:T(8,128)(2,1)}), bf16[1,6,2,128,512]{4,3,2,0,1:T(8,128)(2,1)}) %all-gather.2.cloned.1.call-update) | async-done | bytes 1572880 | tf_op jit(solution)/shard_map/all_gather | solution.py:75
  49.1 1.9 collective-permute-start
  52.3 2.3 collective-permute-done
  54.6 1.7 broadcast_select_fusion
  56.3 3.6 collective-permute-start.1
  59.9 34.9 %collective-permute-done.1 = bf16[6,2,128,512]{3,2,1,0:T(8,128)(2,1)} collective-permute-done((bf16[6,2,128,512]{3,2,1,0:T(8,128)(2,1)S(1)}, bf16[6,2,128,512]{3,2,1,0:T(8,128)(2,1)}, u32[]{:S(2)}, u32[]{:S(2)}) %collective-permute-start.1) | collective-permute-done | bytes 1572896 | tf_op jit(solution)/shard_map/ppermute | solution.py:14
  94.7 1.7 broadcast_select_fusion.1
  96.4 4.6 collective-permute-start.2
  101.0 67.7 %collective-permute-done.2 = bf16[6,2,128,512]{3,2,1,0:T(8,128)(2,1)} collective-permute-done((bf16[6,2,128,512]{3,2,1,0:T(8,128)(2,1)S(1)}, bf16[6,2,128,512]{3,2,1,0:T(8,128)(2,1)}, u32[]{:S(2)}, u32[]{:S(2)}) %collective-permute-start.2) | collective-permute-done | bytes 1572896 | tf_op jit(solution)/shard_map/ppermute | solution.py:14
  169.0 7.9 %collective-permute-start.3 = (bf16[6,2,128,512]{3,2,1,0:T(8,128)(2,1)S(1)}, bf16[6,2,128,512]{3,2,1,0:T(8,128)(2,1)}, u32[]{:S(2)}, u32[]{:S(2)}) collective-permute-start(bf16[6,2,128,512]{3,2,1,0:T(8,128)(2,1)S(1)} %broadcast_select_fusion.2), channel_id=1, source_target_pairs={{0,16},{2,18},{4,20},{6,22},{8,24},{10,26},{12,28},{14,30},{16,0},... | collective-permute-start | bytes 4718600 | tf_op jit(solution)/shard_map/ppermute | solution.py:14
  176.9 68.6 %collective-permute-done.3 = bf16[6,2,128,512]{3,2,1,0:T(8,128)(2,1)} collective-permute-done((bf16[6,2,128,512]{3,2,1,0:T(8,128)(2,1)S(1)}, bf16[6,2,128,512]{3,2,1,0:T(8,128)(2,1)}, u32[]{:S(2)}, u32[]{:S(2)}) %collective-permute-start.3) | collective-permute-done | bytes 1572896 | tf_op jit(solution)/shard_map/ppermute | solution.py:14
  245.5 1.7 broadcast_select_fusion.3
  247.2 1.9 collective-permute-start.4
  249.1 35.6 %collective-permute-done.4 = bf16[6,2,128,512]{3,2,1,0:T(8,128)(2,1)} collective-permute-done((bf16[6,2,128,512]{3,2,1,0:T(8,128)(2,1)S(1)}, bf16[6,2,128,512]{3,2,1,0:T(8,128)(2,1)}, u32[]{:S(2)}, u32[]{:S(2)}) %collective-permute-start.4) | collective-permute-done | bytes 1572896 | tf_op jit(solution)/shard_map/ppermute | solution.py:14
  284.7 1.7 broadcast_select_fusion.4
  286.4 3.4 collective-permute-start.5
  289.8 33.2 %collective-permute-done.5 = bf16[6,2,128,512]{3,2,1,0:T(8,128)(2,1)} collective-permute-done((bf16[6,2,128,512]{3,2,1,0:T(8,128)(2,1)S(1)}, bf16[6,2,128,512]{3,2,1,0:T(8,128)(2,1)}, u32[]{:S(2)}, u32[]{:S(2)}) %collective-permute-start.5) | collective-permute-done | bytes 1572896 | tf_op jit(solution)/shard_map/ppermute | solution.py:14
  323.2 4.3 collective-permute-start.6
  327.6 65.8 %collective-permute-done.6 = bf16[6,2,128,512]{3,2,1,0:T(8,128)(2,1)S(1)} collective-permute-done((bf16[6,2,128,512]{3,2,1,0:T(8,128)(2,1)S(1)}, bf16[6,2,128,512]{3,2,1,0:T(8,128)(2,1)S(1)}, u32[]{:S(2)}, u32[]{:S(2)}) %collective-permute-start.6) | collective-permute-done | bytes 1572896 | tf_op jit(solution)/shard_map/ppermute | solution.py:14
  393.4 1.6 broadcast_select_fusion.6
  395.0 7.4 %collective-permute-start.7 = (bf16[6,2,128,512]{3,2,1,0:T(8,128)(2,1)S(1)}, bf16[6,2,128,512]{3,2,1,0:T(8,128)(2,1)S(1)}, u32[]{:S(2)}, u32[]{:S(2)}) collective-permute-start(bf16[6,2,128,512]{3,2,1,0:T(8,128)(2,1)S(1)} %broadcast_select_fusion.6), channel_id=1, source_target_pairs={{0,256},{2,258},{4,260},{6,262},{8,264},{10,266},{12,268},{14,270}... | collective-permute-start | bytes 4718600 | tf_op jit(solution)/shard_map/ppermute | solution.py:14
  402.4 1.2 cosine_convert_fusion
  403.7 67.5 %collective-permute-done.7 = bf16[6,2,128,512]{3,2,1,0:T(8,128)(2,1)S(1)} collective-permute-done((bf16[6,2,128,512]{3,2,1,0:T(8,128)(2,1)S(1)}, bf16[6,2,128,512]{3,2,1,0:T(8,128)(2,1)S(1)}, u32[]{:S(2)}, u32[]{:S(2)}) %collective-permute-start.7) | collective-permute-done | bytes 1572896 | tf_op jit(solution)/shard_map/ppermute | solution.py:14
  471.6 3.0 copy.9
  474.6 4.3 broadcast_in_dim.8.clone
  478.9 92.4 %while.13 = (s32[]{:T(128)}, f32[128,128,128]{2,1,0:T(8,128)}, bf16[6,2,128,512]{3,2,1,0:T(8,128)(2,1)}, bf16[12,128,512]{1,0,2:T(8,128)(2,1)}, bf16[128,1024]{1...) while((s32[]{:T(128)}, f32[128,128,128]{2,1,0:T(8,128)}, ...), condition=%wide.region_1.2_spmd, body=%wide.region_0.1_spmd.sunk | while | flops 593117184 | bytes 34603184 | solution.py:50
  479.8 0.9 fusion.26
  480.7 2.0 copy.26
  482.7 3.1 convolution_convert_fusion.2
  486.9 1.9 fusion.28
  489.3 1.1 constant_dynamic-update-slice_fusion.2
  491.4 0.9 fusion.26
  492.3 2.0 copy.26
  494.3 3.1 convolution_convert_fusion.2
  498.5 1.9 fusion.28
  500.9 1.1 constant_dynamic-update-slice_fusion.2
  502.9 0.9 fusion.26
  503.8 2.0 copy.26
  505.8 3.1 convolution_convert_fusion.2
  510.0 1.9 fusion.28
  512.4 1.1 constant_dynamic-update-slice_fusion.2
  514.4 0.9 fusion.26
  515.4 2.0 copy.26
  517.3 3.1 convolution_convert_fusion.2
  521.5 1.9 fusion.28
  523.9 1.1 constant_dynamic-update-slice_fusion.2
  526.0 0.9 fusion.26
  526.9 2.0 copy.26
  528.9 3.1 convolution_convert_fusion.2
  533.1 1.9 fusion.28
  535.5 1.1 constant_dynamic-update-slice_fusion.2
  538.5 2.0 copy.26
  540.5 3.1 convolution_convert_fusion.2
  544.7 1.9 fusion.28
  547.1 1.1 constant_dynamic-update-slice_fusion.2
  550.0 2.0 copy.26
  552.0 3.1 convolution_convert_fusion.2
  556.2 1.9 fusion.28
  558.6 1.1 constant_dynamic-update-slice_fusion.2
  561.6 2.0 copy.26
  563.6 3.1 convolution_convert_fusion.2
  567.8 1.9 fusion.28
  570.2 1.2 constant_dynamic-update-slice_fusion.2
  571.3 6.6 %fusion.3 = bf16[1,1,128,128,128]{4,3,2,1,0:T(8,128)(2,1)} fusion(f32[128,128,128]{2,1,0:T(8,128)} %get-tuple-element.99), kind=kLoop, calls=%fused_computation.10 | loop fusion | flops 4194304 | bytes 12582912 | tf_op jit(solution)/shard_map/broadcast_in_dim | solution.py:81
  (57 shorter events, 25.3 us)
Async XLA Ops:
  6.5 44.5 %copy-start = (s32[2,1]{0,1:T(1,128)S(1)}, s32[2,1]{0,1:T(1,128)}, u32[]{:S(2)}) copy-start(s32[2,1]{0,1:T(1,128)} %param.5) | copy-start | bytes 28
  6.5 42.6 %all-gather.2.cloned.1.call-start = ((), (), s32[]{:S(2)}) async-start(), calls=%async_computation | async-start | bytes 2359296 | tf_op jit(solution)/shard_map/all_gather | solution.py:75
  49.1 5.5 collective-permute-start
  56.3 38.4 %collective-permute-start.1 = (bf16[6,2,128,512]{3,2,1,0:T(8,128)(2,1)S(1)}, bf16[6,2,128,512]{3,2,1,0:T(8,128)(2,1)}, u32[]{:S(2)}, u32[]{:S(2)}) collective-permute-start(bf16[6,2,128,512]{3,2,1,0:T(8,128)(2,1)S(1)} %broadcast_select_fusion), channel_id=1, source_target_pairs={{0,4},{2,6},{4,0},{6,2},{8,12},{10,14},{12,8},{14,10},{16,20},{18,... | collective-permute-start | bytes 4718600 | tf_op jit(solution)/shard_map/ppermute | solution.py:14
  96.4 72.3 %collective-permute-start.2 = (bf16[6,2,128,512]{3,2,1,0:T(8,128)(2,1)S(1)}, bf16[6,2,128,512]{3,2,1,0:T(8,128)(2,1)}, u32[]{:S(2)}, u32[]{:S(2)}) collective-permute-start(bf16[6,2,128,512]{3,2,1,0:T(8,128)(2,1)S(1)} %broadcast_select_fusion.1), channel_id=1, source_target_pairs={{0,8},{2,10},{4,12},{6,14},{8,0},{10,2},{12,4},{14,6},{16,24},{18,... | collective-permute-start | bytes 4718600 | tf_op jit(solution)/shard_map/ppermute | solution.py:14
  169.0 76.6 %collective-permute-start.3 = (bf16[6,2,128,512]{3,2,1,0:T(8,128)(2,1)S(1)}, bf16[6,2,128,512]{3,2,1,0:T(8,128)(2,1)}, u32[]{:S(2)}, u32[]{:S(2)}) collective-permute-start(bf16[6,2,128,512]{3,2,1,0:T(8,128)(2,1)S(1)} %broadcast_select_fusion.2), channel_id=1, source_target_pairs={{0,16},{2,18},{4,20},{6,22},{8,24},{10,26},{12,28},{14,30},{16,0},... | collective-permute-start | bytes 4718600 | tf_op jit(solution)/shard_map/ppermute | solution.py:14
  247.2 37.5 %collective-permute-start.4 = (bf16[6,2,128,512]{3,2,1,0:T(8,128)(2,1)S(1)}, bf16[6,2,128,512]{3,2,1,0:T(8,128)(2,1)}, u32[]{:S(2)}, u32[]{:S(2)}) collective-permute-start(bf16[6,2,128,512]{3,2,1,0:T(8,128)(2,1)S(1)} %broadcast_select_fusion.3), channel_id=1, source_target_pairs={{0,32},{2,34},{4,36},{6,38},{8,40},{10,42},{12,44},{14,46},{16,48}... | collective-permute-start | bytes 4718600 | tf_op jit(solution)/shard_map/ppermute | solution.py:14
  286.4 36.6 %collective-permute-start.5 = (bf16[6,2,128,512]{3,2,1,0:T(8,128)(2,1)S(1)}, bf16[6,2,128,512]{3,2,1,0:T(8,128)(2,1)}, u32[]{:S(2)}, u32[]{:S(2)}) collective-permute-start(bf16[6,2,128,512]{3,2,1,0:T(8,128)(2,1)S(1)} %broadcast_select_fusion.4), channel_id=1, source_target_pairs={{0,64},{2,66},{4,68},{6,70},{8,72},{10,74},{12,76},{14,78},{16,80}... | collective-permute-start | bytes 4718600 | tf_op jit(solution)/shard_map/ppermute | solution.py:14
  323.2 4.3 copy-start.1
  323.2 70.2 %collective-permute-start.6 = (bf16[6,2,128,512]{3,2,1,0:T(8,128)(2,1)S(1)}, bf16[6,2,128,512]{3,2,1,0:T(8,128)(2,1)S(1)}, u32[]{:S(2)}, u32[]{:S(2)}) collective-permute-start(bf16[6,2,128,512]{3,2,1,0:T(8,128)(2,1)S(1)} %broadcast_select_fusion.5), channel_id=1, source_target_pairs={{0,128},{2,130},{4,132},{6,134},{8,136},{10,138},{12,140},{14,142}... | collective-permute-start | bytes 4718600 | tf_op jit(solution)/shard_map/ppermute | solution.py:14
  395.0 76.1 %collective-permute-start.7 = (bf16[6,2,128,512]{3,2,1,0:T(8,128)(2,1)S(1)}, bf16[6,2,128,512]{3,2,1,0:T(8,128)(2,1)S(1)}, u32[]{:S(2)}, u32[]{:S(2)}) collective-permute-start(bf16[6,2,128,512]{3,2,1,0:T(8,128)(2,1)S(1)} %broadcast_select_fusion.6), channel_id=1, source_target_pairs={{0,256},{2,258},{4,260},{6,262},{8,264},{10,266},{12,268},{14,270}... | collective-permute-start | bytes 4718600 | tf_op jit(solution)/shard_map/ppermute | solution.py:14
Sparse Core Ops, SparseCore 0:
  9.4 39.6 all-gather.1
where the time goes:
time: 586 us; the launch traced here: 585 us
  waiting for transfers between devices  418 us (71%)
  local copies, waits for them, and re-layouts  49.9 us (9%)
  matrix products  39.8 us (7%)
  starting transfers between devices  35 us (6%)
  other arithmetic  27.4 us (5%)
  between operations  14.2 us (2%)
    ppermute x8, waiting for transfers between devices, swapped(): return lax.ppermute(value, axis, pairs)  376 us
    all_gather x1, waiting for transfers between devices, per_device(): all_groups = lax.all_gather(spectra, 'seg', axis=1, tiled=True)[0]  41.9 us
    ppermute x8, starting transfers between devices, swapped(): return lax.ppermute(value, axis, pairs)  35 us
    dot_general x8, matrix products, one_slab(): jnp.einsum('sif,sjf->fij', left_both, right_both, preferred_element_type=...  24.6 us
    concatenate x8, local copies, waits for them, and re-layouts, one_slab(): left_both = jnp.concatenate([plain_rows, turned_rows], axis=1)  15.8 us
    dot_general x8, matrix products, one_slab(): jnp.dot(table_matrix, spectrum, preferred_element_type=jnp.float32)  15.1 us
    dynamic_update_slice x16, local copies, waits for them, and re-layouts, one_slab(): return lax.dynamic_update_slice_in_dim(collected, lag_part, first, 1)  13.1 us
  transfers between devices with their start and end apart: 9, of which 9 were waited for; matrix products, arithmetic and copies ran while one was open for 0% of the time, Pallas kernels for 0%

commit v1 on v0

--- a/solution.py
+++ b/solution.py
@@ -1,17 +1,151 @@
+import functools
 import math
 
 import jax
 import jax.numpy as jnp
+import numpy as np
 from jax import lax
+from jax.experimental import pallas as pl
+from jax.experimental.pallas import tpu as pltpu
 from jax.sharding import PartitionSpec as P
 
 LAGS = 128
-
-
-def swapped(value, axis, bit):
-    mask = 2**bit
-    pairs = [(source, source ^ mask) for source in range(lax.axis_size(axis))]
-    return lax.ppermute(value, axis, pairs)
+MESH = pl.DeviceIdType.MESH
+RING = 8
+CHUNKS = 8
+SLOTS = 2 * CHUNKS + 2
+STREAMS = 2
+ROWS = 768
+PIECE = ROWS // (STREAMS * CHUNKS)
+
+
+def path(mask, place):
+    ahead = ((place ^ mask) - place) % RING
+    first = ((place >> 1) & 1) if mask == 5 else 0
+    return (0, ahead, first) if ahead <= 4 else (1, RING - ahead, first)
+
+
+def ring_table():
+    table = np.zeros((RING, RING, 16), np.int32)
+    for mask in range(RING):
+        for place in range(RING):
+            row = table[mask, place]
+            if mask == 0:
+                row[8:10] = 8
+            elif mask == 4:
+                row[0], row[6], row[8], row[9] = 1, 1, 3, 7
+            else:
+                direction, _, first = path(mask, place)
+                row[direction * 4 + first], row[direction * 4 + first + 2] = 1, 1
+                back, hops, start = path(mask, place ^ mask)
+                row[8:10] = back * 4 + start + hops - 1
+    return table.reshape(-1)
+
+
+def ring_kernel(plan_ref, table_ref, near_ref, far_ref, out_ref, middle, landed, staged, send_sem, recv_sem):
+    ch, seg = lax.axis_index("ch"), lax.axis_index("seg")
+    z, y = ch // 2 % RING, ch // 32
+    targets = [
+        (ch + 32) % 256,
+        (ch + 224) % 256,
+        ch - z * 2 + (z + 1) % RING * 2,
+        ch - z * 2 + (z + RING - 1) % RING * 2,
+    ]
+    mask = plan_ref[seg, 0] ^ ch
+    bases = [(((mask // 32) % RING) * RING + y) * 16, (((mask // 2) % RING) * RING + z) * 16]
+
+    barrier = pltpu.get_barrier_semaphore()
+    for target in targets:
+        pl.semaphore_signal(barrier, inc=1, device_id=(target, seg), device_id_type=MESH)
+    pl.semaphore_wait(barrier, 4)
+
+    halves = (near_ref, far_ref)
+    for stage in range(2):
+        source = halves if stage == 0 else (middle.at[0], middle.at[1])
+        goal = (middle.at[0], middle.at[1]) if stage == 0 else (out_ref.at[0], out_ref.at[1])
+
+        def rows(stream, chunk):
+            return pl.ds(pl.multiple_of(stream * (ROWS // STREAMS) + chunk * PIECE, 16), PIECE)
+
+        def copy(link, stream, slot, stage=stage):
+            return pltpu.make_async_remote_copy(
+                src_ref=staged.at[link, stream, slot % 2],
+                dst_ref=landed.at[stage, link, stream, slot],
+                send_sem=send_sem.at[link, stream, slot % 2],
+                recv_sem=recv_sem.at[stage, link, stream, slot],
+                device_id=(targets[link], seg),
+                device_id_type=MESH,
+            )
+
+        def send(slot, first=False, second=False, stage=stage, source=source):
+            for stream in range(STREAMS):
+                for dim in range(2):
+                    chunk = jnp.minimum(slot // 2, CHUNKS - 1)
+                    own = source[dim ^ stage][rows(stream, chunk), :]
+                    for direction in range(2):
+                        link = 2 * dim + direction
+                        value = own
+                        if not first:
+                            copy(link, stream, slot - 1).wait_recv()
+                            if not second:
+                                copy(link, stream, slot - 2).wait_send()
+                            flag = table_ref[bases[dim] + direction * 4 + slot % 4]
+                            value = jnp.where(flag == 1, own, landed[stage, link, stream, slot - 1])
+                        staged[link, stream, slot % 2] = value
+                        copy(link, stream, slot).start()
+
+        def pick(chunk, stage=stage, source=source, goal=goal):
+            for dim in range(2):
+                code = table_ref[bases[dim] + 8 + chunk % 2]
+                for stream in range(STREAMS):
+                    value = source[dim ^ stage][rows(stream, chunk), :]
+                    for place in range(8):
+                        found = landed[stage, 2 * dim + place // 4, stream, 2 * chunk + place % 4]
+                        value = jnp.where(code == place, found, value)
+                    goal[dim ^ stage][rows(stream, chunk), :] = value
+
+        send(0, first=True)
+        send(1, second=True)
+
+        def pair(number, carry, send=send, pick=pick):
+            send(2 * number)
+
+            @pl.when(number >= 2)
+            def _():
+                pick(number - 2)
+
+            send(2 * number + 1)
+            return carry
+
+        lax.fori_loop(1, SLOTS // 2, pair, 0)
+        for link in range(4):
+            for stream in range(STREAMS):
+                copy(link, stream, SLOTS - 1).wait_recv()
+                copy(link, stream, SLOTS - 2).wait_send()
+                copy(link, stream, SLOTS - 1).wait_send()
+        pick(CHUNKS - 1)
+
+
+def ring_move(plan, near, far):
+    width = near.shape[-1]
+    vmem = pl.BlockSpec(memory_space=pltpu.VMEM)
+    smem = pl.BlockSpec(memory_space=pltpu.SMEM)
+    return pl.pallas_call(
+        ring_kernel,
+        out_shape=jax.ShapeDtypeStruct((2, ROWS, width), jnp.bfloat16),
+        in_specs=[smem, smem, vmem, vmem],
+        out_specs=vmem,
+        scratch_shapes=[
+            pltpu.VMEM((2, ROWS, width), jnp.bfloat16),
+            pltpu.VMEM((2, 4, STREAMS, SLOTS, PIECE, width), jnp.bfloat16),
+            pltpu.VMEM((4, STREAMS, 2, PIECE, width), jnp.bfloat16),
+            pltpu.SemaphoreType.DMA((4, STREAMS, 2)),
+            pltpu.SemaphoreType.DMA((2, 4, STREAMS, SLOTS)),
+        ],
+        compiler_params=pltpu.CompilerParams(
+            collective_id=0, has_side_effects=True, vmem_limit_bytes=48 * 2**20
+        ),
+    )(plan, jnp.asarray(ring_table()), near.reshape(ROWS, width), far.reshape(ROWS, width))
 
 
 def lag_table(bin_count, lag_count):
@@ -50,34 +184,24 @@
     return lax.fori_loop(0, channels // row_block, one_slab, start_value)
 
 
-def route_block(block_data, partner_mask):
-    bit_count = lax.axis_size("ch").bit_length() - 1
-    bit_order = list(range(bit_count))
-    for bit_number in bit_order:
-
-        def move(current, bit_number=bit_number):
-            return swapped(current, "ch", bit_number)
-
-        taken = jnp.bitwise_and(jnp.right_shift(partner_mask, bit_number), 1) == 1
-        arrived = move(block_data)
-        block_data = jnp.where(taken, arrived, block_data)
-    return block_data
+def swapped(value, bit):
+    return lax.ppermute(value, "ch", [(block, block ^ bit) for block in range(lax.axis_size("ch"))])
 
 
 def per_device(spectra, plan):
-    mine_block = spectra[0]
-    seg_dev = mine_block.shape[0]
-    bin_count = mine_block.shape[3]
+    mine = spectra[0]
+    seg_dev, bin_count = mine.shape[0], mine.shape[3]
     table_matrix = lag_table(bin_count, LAGS)
     group_count = lax.axis_size("seg")
     factor = 1.0 / math.sqrt(2.0 * seg_dev * group_count * bin_count)
-    position = lax.axis_index("ch")
-    all_groups = lax.all_gather(spectra, "seg", axis=1, tiled=True)[0]
-    my_round = lax.axis_index("seg")
-    round_entry = lax.dynamic_index_in_dim(plan[:, 0], my_round, keepdims=False)
-    partner_mask = jnp.bitwise_xor(round_entry, position)
-    partner_block = route_block(all_groups, partner_mask)
-    lags_now = correlate(all_groups, partner_block, table_matrix)
+    entry = lax.dynamic_index_in_dim(plan[:, 0], lax.axis_index("seg"), keepdims=False)
+    mask = jnp.bitwise_xor(entry, lax.axis_index("ch"))
+    others = lax.ppermute(mine, "seg", [(0, 1), (1, 0)])
+    left = jnp.concatenate([mine, others], axis=0)
+    moved = jnp.where(mask & 16 == 16, swapped(left, 16), left)
+    moved = jnp.where(mask & 1 == 1, swapped(moved, 1), moved)
+    right = ring_move(plan, moved[:seg_dev], moved[seg_dev:]).reshape(left.shape)
+    lags_now = correlate(left, right, table_matrix)
     return (lags_now * factor).astype(jnp.bfloat16)[None, None]
 
 

time: 586 us -> 327 us (0.56)
  waiting for transfers between devices: 418 us -> 55.1 us
  Pallas kernels: 0 us -> 148 us
  starting transfers between devices: 35 us -> 8.08 us
  between operations: 14.2 us -> 0.77 us
    ppermute x8 -> x3, waiting for transfers between devices: 376 us -> 55.1 us  [the longest x2 35.5 us: swapped(): lax.ppermute(value, 'ch', [(block, block ^ bit) for block in range(lax.ax...]
    pallas_call x0 -> x1, Pallas kernels: none -> 148 us  [ring_move(): pl.pallas_call(ring_kernel, out_shape=jax.ShapeDtypeStruct((2, ROWS, widt...]
    all_gather x1 -> x0, waiting for transfers between devices: 41.9 us -> none  [per_device(): all_groups = lax.all_gather(spectra, 'seg', axis=1, tiled=True)[0]]
    ppermute x8 -> x3, starting transfers between devices: 35 us -> 8.08 us  [the longest x2 4.65 us: swapped(): lax.ppermute(value, 'ch', [(block, block ^ bit) for block in range(lax.ax...]
    select_n x8 -> x2, other arithmetic: 8.92 us -> 1.78 us  [the longest x1 1.61 us: per_device(): moved = jnp.where(mask & 16 == 16, swapped(left, 16), left)]
  transfers between devices with their start and end apart: 9 -> 3, of which waited for: 9 -> 3; matrix products, arithmetic and copies ran while one was open for 0% -> 1% of each run, Pallas kernels for 0% -> 0%
where the time goes in v1:
time: 327 us; the launch traced here: 326 us
  Pallas kernels  148 us (45%)
  waiting for transfers between devices  55.1 us (17%)
  local copies, waits for them, and re-layouts  49.1 us (15%)
  matrix products  39.6 us (12%)
  other arithmetic  24.7 us (8%)
  starting transfers between devices  8.08 us (2%)
    pallas_call x1, Pallas kernels, ring_move(): pl.pallas_call(ring_kernel, out_shape=jax.ShapeDtypeStruct((2, ROWS, widt...  148 us
    ppermute x2, waiting for transfers between devices, swapped(): lax.ppermute(value, 'ch', [(block, block ^ bit) for block in range(lax.ax...  35.5 us
    dot_general x8, matrix products, one_slab(): jnp.einsum('sif,sjf->fij', left_both, right_both, preferred_element_type=...  24.6 us
    ppermute x1, waiting for transfers between devices, per_device(): others = lax.ppermute(mine, 'seg', [(0, 1), (1, 0)])  19.6 us
    concatenate x8, local copies, waits for them, and re-layouts, one_slab(): left_both = jnp.concatenate([plain_rows, turned_rows], axis=1)  15.8 us
    dot_general x8, matrix products, one_slab(): jnp.dot(table_matrix, spectrum, preferred_element_type=jnp.float32)  15 us
    dynamic_update_slice x16, local copies, waits for them, and re-layouts, one_slab(): return lax.dynamic_update_slice_in_dim(collected, lag_part, first, 1)  13.1 us
    neg x8, other arithmetic, one_slab(): turned_rows = jnp.concatenate([row_slab[:, 1], -row_slab[:, 0]], axis=0)  7.29 us
  transfers between devices with their start and end apart: 3, of which 3 were waited for; matrix products, arithmetic and copies ran while one was open for 1% of the time, Pallas kernels for 0%

profile of v1, /device:TPU:6, one launch (start us, length us, event | category | flops | bytes accessed | tf_op | source)
XLA Modules:
  0.0 325.7 jit_solution(5538585406186030031)
XLA Ops:
  0.0 3.4 %collective-permute-start = (bf16[3,2,128,512]{3,2,1,0:T(8,128)(2,1)}, bf16[3,2,128,512]{3,2,1,0:T(8,128)(2,1)S(1)}, u32[]{:S(2)}, u32[]{:S(2)}) collective-permute-start(bf16[3,2,128,512]{3,2,1,0:T(8,128)(2,1)} %bitcast.49), channel_id=1, source_target_pairs={{0,1},{1,0},{2,3},{3,2},{4,5},{5,4},{6,7},{7,6},{8,9},{9,8},{10,11... | collective-permute-start | bytes 2359304 | tf_op jit(solution)/shard_map/ppermute | solution.py:199
  3.4 19.6 %collective-permute-done = bf16[3,2,128,512]{3,2,1,0:T(8,128)(2,1)S(1)} collective-permute-done((bf16[3,2,128,512]{3,2,1,0:T(8,128)(2,1)}, bf16[3,2,128,512]{3,2,1,0:T(8,128)(2,1)S(1)}, u32[]{:S(2)}, u32[]{:S(2)}) %collective-permute-start) | collective-permute-done | bytes 786464 | tf_op jit(solution)/shard_map/ppermute | solution.py:199
  23.0 2.5 pad_maximum_fusion.2
  25.5 2.7 collective-permute-start.1
  29.5 33.5 %collective-permute-done.1 = bf16[6,2,128,512]{3,2,1,0:T(8,128)(2,1)} collective-permute-done((bf16[6,2,128,512]{3,2,1,0:T(8,128)(2,1)}, bf16[6,2,128,512]{3,2,1,0:T(8,128)(2,1)}, u32[]{:S(2)}, u32[]{:S(2)}) %collective-permute-start.1) | collective-permute-done | bytes 1572896 | tf_op jit(solution)/shard_map/ppermute | solution.py:188
  62.9 1.6 broadcast_select_fusion
  64.6 1.9 collective-permute-start.2
  66.6 1.2 cosine_convert_fusion
  67.8 2.0 collective-permute-done.2
  70.7 148.0 %shard_map.37 = bf16[2,768,512]{2,1,0:T(8,128)(2,1)S(1)} custom-call(s32[2,1]{1,0:T(2,128)S(1)} %copy.12.plan_ref, s32[1024]{0:T(1024)S(1)} %copy-done, bf16[768,512]{1,0:T(8,128)(2,1)S(1)} %bitcast.44, bf16[768,512]{1,0:T(8,128)(2,1)S(1)} %bitcast.43), custom_call_target="tpu_custom_call" | custom-call | tf_op jit(solution)/shard_map/pallas_call | solution.py:133
  218.9 0.8 copy.20
  219.6 0.8 copy.21
  220.4 2.1 pad_maximum_fusion.1
  222.5 4.3 %broadcast_in_dim.8.clone = f32[128,128,128]{2,1,0:T(8,128)} broadcast(f32[]{:T(128)} %constant.62.clone.1), dimensions={} | broadcast | bytes 8388612 | tf_op jit(solution)/shard_map/broadcast_in_dim | solution.py:183
  226.8 92.3 %while.13 = (s32[]{:T(128)}, f32[128,128,128]{2,1,0:T(8,128)}, bf16[6,2,128,512]{3,2,1,0:T(8,128)(2,1)}, bf16[12,128,512]{1,0,2:T(8,128)(2,1)}, bf16[128,1024]{1...) while((s32[]{:T(128)}, f32[128,128,128]{2,1,0:T(8,128)}, ...), condition=%wide.region_1.2_spmd, body=%wide.region_0.1_spmd.sunk | while | flops 593117184 | bytes 34603184 | solution.py:184
  226.8 0.9 dynamic-slice_bitcast_fusion.4
  227.7 0.9 fusion.28
  228.6 2.0 copy.33
  230.6 3.1 convolution_convert_fusion.2
  234.8 1.9 fusion.30
  237.2 1.2 constant_dynamic-update-slice_fusion.2
  238.3 0.9 dynamic-slice_bitcast_fusion.4
  239.2 0.9 fusion.28
  240.2 2.0 copy.33
  242.2 3.1 convolution_convert_fusion.2
  246.3 1.9 fusion.30
  248.7 1.1 constant_dynamic-update-slice_fusion.2
  249.9 0.9 dynamic-slice_bitcast_fusion.4
  250.8 0.9 fusion.28
  251.7 2.0 copy.33
  253.7 3.1 convolution_convert_fusion.2
  257.9 1.9 fusion.30
  260.3 1.1 constant_dynamic-update-slice_fusion.2
  261.4 0.9 dynamic-slice_bitcast_fusion.4
  262.3 0.9 fusion.28
  263.3 2.0 copy.33
  265.2 3.1 convolution_convert_fusion.2
  269.4 1.9 fusion.30
  271.8 1.2 constant_dynamic-update-slice_fusion.2
  273.0 0.9 dynamic-slice_bitcast_fusion.4
  273.9 0.9 fusion.28
  274.8 2.0 copy.33
  276.8 3.1 convolution_convert_fusion.2
  281.0 1.9 fusion.30
  283.4 1.1 constant_dynamic-update-slice_fusion.2
  284.5 0.9 dynamic-slice_bitcast_fusion.4
  285.4 0.9 fusion.28
  286.4 2.0 copy.33
  288.3 3.1 convolution_convert_fusion.2
  292.5 1.9 fusion.30
  294.9 1.1 constant_dynamic-update-slice_fusion.2
  296.0 0.9 dynamic-slice_bitcast_fusion.4
  296.9 0.9 fusion.28
  297.8 2.0 copy.33
  299.8 3.1 convolution_convert_fusion.2
  304.0 1.9 fusion.30
  306.4 1.1 constant_dynamic-update-slice_fusion.2
  307.5 0.9 dynamic-slice_bitcast_fusion.4
  308.4 0.9 fusion.28
  309.4 2.0 copy.33
  311.4 3.1 convolution_convert_fusion.2
  315.5 1.9 fusion.30
  317.9 1.1 constant_dynamic-update-slice_fusion.2
  319.0 6.6 %fusion.3 = bf16[1,1,128,128,128]{4,3,2,1,0:T(8,128)(2,1)} fusion(f32[128,128,128]{2,1,0:T(8,128)} %get-tuple-element.99), kind=kLoop, calls=%fused_computation.10 | loop fusion | flops 4194304 | bytes 12582912 | tf_op jit(solution)/shard_map/broadcast_in_dim | solution.py:205
  (45 shorter events, 14.7 us)
Async XLA Ops:
  0.0 62.9 %copy-start.1 = (bf16[1,3,2,128,512]{4,3,2,1,0:T(8,128)(2,1)S(1)}, bf16[1,3,2,128,512]{4,3,2,1,0:T(8,128)(2,1)}, u32[]{:S(2)}) copy-start(bf16[1,3,2,128,512]{4,3,2,1,0:T(8,128)(2,1)} %param.5) | copy-start | bytes 2359300
  0.0 28.2 %copy-start.2 = (s32[2,1]{0,1:T(1,128)S(1)}, s32[2,1]{0,1:T(1,128)}, u32[]{:S(2)}) copy-start(s32[2,1]{0,1:T(1,128)} %param.6) | copy-start | bytes 28
  0.0 23.0 %collective-permute-start = (bf16[3,2,128,512]{3,2,1,0:T(8,128)(2,1)}, bf16[3,2,128,512]{3,2,1,0:T(8,128)(2,1)S(1)}, u32[]{:S(2)}, u32[]{:S(2)}) collective-permute-start(bf16[3,2,128,512]{3,2,1,0:T(8,128)(2,1)} %bitcast.49), channel_id=1, source_target_pairs={{0,1},{1,0},{2,3},{3,2},{4,5},{5,4},{6,7},{7,6},{8,9},{9,8},{10,11... | collective-permute-start | bytes 2359304 | tf_op jit(solution)/shard_map/ppermute | solution.py:199
  25.5 37.5 %collective-permute-start.1 = (bf16[6,2,128,512]{3,2,1,0:T(8,128)(2,1)}, bf16[6,2,128,512]{3,2,1,0:T(8,128)(2,1)}, u32[]{:S(2)}, u32[]{:S(2)}) collective-permute-start(bf16[6,2,128,512]{3,2,1,0:T(8,128)(2,1)} %pad_maximum_fusion.2), channel_id=1, source_target_pairs={{0,32},{2,34},{4,36},{6,38},{8,40},{10,42},{12,44},{14,46},{16,48}... | collective-permute-start | bytes 4718600 | tf_op jit(solution)/shard_map/ppermute | solution.py:188
  64.6 5.3 %collective-permute-start.2 = (bf16[6,2,128,512]{3,2,1,0:T(8,128)(2,1)S(1)}, bf16[6,2,128,512]{3,2,1,0:T(8,128)(2,1)S(1)}, u32[]{:S(2)}, u32[]{:S(2)}) collective-permute-start(bf16[6,2,128,512]{3,2,1,0:T(8,128)(2,1)S(1)} %broadcast_select_fusion), channel_id=1, source_target_pairs={{0,2},{2,0},{4,6},{6,4},{8,10},{10,8},{12,14},{14,12},{16,18},{18,... | collective-permute-start | bytes 4718600 | tf_op jit(solution)/shard_map/ppermute | solution.py:188
  70.0 0.7 copy-start

commit v2 on v1

--- a/solution.py
+++ b/solution.py
@@ -12,9 +12,9 @@
 LAGS = 128
 MESH = pl.DeviceIdType.MESH
 RING = 8
-CHUNKS = 8
+CHUNKS = 4
 SLOTS = 2 * CHUNKS + 2
-STREAMS = 2
+STREAMS = 4
 ROWS = 768
 PIECE = ROWS // (STREAMS * CHUNKS)
 
@@ -148,40 +148,149 @@
     )(plan, jnp.asarray(ring_table()), near.reshape(ROWS, width), far.reshape(ROWS, width))
 
 
-def lag_table(bin_count, lag_count):
-    bin_index = jnp.arange(bin_count, dtype=jnp.int32)
-    lag_index = jnp.arange(lag_count, dtype=jnp.int32) - lag_count // 2
-    product = lag_index[:, None] * bin_index[None, :] % (2 * bin_count)
-    angles = product.astype(jnp.float32) * (jnp.pi / bin_count)
-    return jnp.concatenate([jnp.cos(angles), -jnp.sin(angles)], axis=1).astype(jnp.bfloat16)
-
-
-def correlate(left_spec, right_spec, table_matrix):
-    channels = left_spec.shape[2]
-    bin_count = left_spec.shape[3]
-    lag_count = table_matrix.shape[0]
-    row_block = min(channels, 16)
-    right_both = jnp.concatenate([right_spec[:, 0], right_spec[:, 1]], axis=0)
-
-    def one_slab(number, collected):
-        first = number * row_block
-        row_slab = lax.dynamic_slice_in_dim(left_spec, first, row_block, 2)
-        plain_rows = jnp.concatenate([row_slab[:, 0], row_slab[:, 1]], axis=0)
-        turned_rows = jnp.concatenate([row_slab[:, 1], -row_slab[:, 0]], axis=0)
-        left_both = jnp.concatenate([plain_rows, turned_rows], axis=1)
-        both_parts = jnp.einsum(
-            "sif,sjf->fij", left_both, right_both, preferred_element_type=jnp.float32
-        ).astype(jnp.bfloat16)
-        spectrum = jnp.concatenate(
-            [both_parts[:, :row_block], both_parts[:, row_block:]], axis=0
-        ).reshape(2 * bin_count, row_block * channels)
-        lag_part = jnp.dot(table_matrix, spectrum, preferred_element_type=jnp.float32).reshape(
-            lag_count, row_block, channels
-        )
-        return lax.dynamic_update_slice_in_dim(collected, lag_part, first, 1)
-
-    start_value = jnp.zeros((lag_count, channels, channels), jnp.float32)
-    return lax.fori_loop(0, channels // row_block, one_slab, start_value)
+BINS = 512
+SEGMENTS = 6
+CHANNELS = 128
+WINDOWS = 8
+TONES = 128
+SPAN = 2 * TONES
+
+
+def window_tables():
+    time = np.arange(1024)
+    bins = np.arange(BINS)
+    angle = 2 * np.pi * (np.outer(time, bins) % 1024) / 1024
+    weight = np.where(bins == 0, np.sqrt(0.5), 1.0)
+    samples = np.concatenate([np.cos(angle) * weight, -np.sin(angle) * weight], axis=1)
+    tones = 2 * np.pi * (np.arange(TONES) + 0.5) / SPAN
+
+    def table(offsets):
+        turn = np.exp(-1j * np.outer(tones, offsets))
+        result = np.empty((TONES, 2, WINDOWS, 2 * BINS))
+        for window in range(WINDOWS):
+            both = turn @ samples[(window * 128 + offsets) % 1024]
+            result[:, 0, window], result[:, 1, window] = both.real, both.imag
+        return (result / 32.0).reshape(TONES * 2 * WINDOWS, 2 * BINS)
+
+    return table(np.arange(-64, 192)), table(np.arange(128))
+
+
+def lag_tables():
+    tones = 2 * np.pi * (np.arange(TONES // 2) + 0.5) / SPAN
+    scale = 1024.0 / BINS * 2.0 / SPAN / math.sqrt(2.0 * SEGMENTS * BINS)
+    even, late, odd = np.arange(0, 65, 2), np.arange(2, 65, 2), np.arange(1, 64, 2)
+    parts = [np.cos(np.outer(even, tones)), np.sin(np.outer(late, tones))]
+    parts += [np.cos(np.outer(odd, tones)), np.sin(np.outer(odd, tones))]
+    return np.kron(np.concatenate(parts, axis=0) * scale, np.eye(8))
+
+
+def correlate_kernel(left_table, right_table, lag_table, left_near, left_far, right_near, right_far, out_ref,
+                     left_turned, right_turned, left_tones, right_tones, folded, constant):
+    f32, bf16 = jnp.float32, jnp.bfloat16
+
+    def block(near, far, segment, part):
+        source = near if segment < 3 else far
+        first = (segment % 3) * 2 * CHANNELS + part * CHANNELS
+        return source[first:first + CHANNELS, :]
+
+    for segment in range(SEGMENTS):
+        lanes = slice(segment * CHANNELS, (segment + 1) * CHANNELS)
+        for part in range(2):
+            rows = slice(part * BINS, (part + 1) * BINS)
+            left_turned[rows, lanes] = block(left_near, left_far, segment, part).T
+            right_turned[rows, lanes] = block(right_near, right_far, segment, part).T
+
+    first_lane = lax.broadcasted_iota(jnp.int32, (CHANNELS, 128), 1) == 0
+    total = jnp.zeros((CHANNELS, CHANNELS), f32)
+    for segment in range(SEGMENTS):
+        mine = jnp.where(first_lane, block(left_near, left_far, segment, 1)[:, :128].astype(f32), 0.0).astype(bf16)
+        theirs = block(right_near, right_far, segment, 1)[:, :128]
+        total += lax.dot_general(mine, theirs, (((1,), (1,)), ((), ())), preferred_element_type=f32)
+    constant[...] = total * (1.0 / math.sqrt(2.0 * SEGMENTS * BINS))
+
+    step = 256
+
+    def tones_of(number, carry):
+        rows = pl.ds(pl.multiple_of(number * step, step), step)
+        where = pl.ds(number * (step // 16), step // 16)
+        left = jnp.dot(left_table[rows, :], left_turned[...], preferred_element_type=f32)
+        right = jnp.dot(right_table[rows, :], right_turned[...], preferred_element_type=f32)
+        for segment in range(SEGMENTS):
+            lanes = slice(segment * CHANNELS, (segment + 1) * CHANNELS)
+            depth = slice(segment * 16, (segment + 1) * 16)
+            left_tones[where, depth, :] = left[:, lanes].reshape(step // 16, 16, CHANNELS).astype(bf16)
+            plain = right[:, lanes].reshape(step // 16, 2, 8, CHANNELS)
+            right_tones[where, depth, :CHANNELS] = plain.reshape(step // 16, 16, CHANNELS).astype(bf16)
+            turned = jnp.concatenate([-plain[:, 1], plain[:, 0]], axis=1)
+            right_tones[where, depth, CHANNELS:] = turned.astype(bf16)
+        return carry
+
+    lax.fori_loop(0, TONES * 16 // step, tones_of, 0)
+
+    def cross(tone):
+        return jnp.dot(left_tones[tone].T, right_tones[tone], preferred_element_type=f32)
+
+    def fold(number, carry):
+        tone = number * 2
+        pairs = []
+        for offset in range(2):
+            low, high = cross(tone + offset), cross(TONES - 1 - tone - offset)
+            plus, minus = low + high, low - high
+            pairs.append((plus[:, :128], minus[:, 128:], minus[:, :128], plus[:, 128:]))
+        rows = pl.ds(pl.multiple_of(number * 16, 16), 16)
+        for kind in range(4):
+            one, two = pairs[0][kind], pairs[1][kind]
+            for group in range(16):
+                both = jnp.concatenate([one[group * 8:group * 8 + 8], two[group * 8:group * 8 + 8]], axis=0)
+                lanes = slice((group % 2) * 128, (group % 2) * 128 + 128)
+                folded[kind, group // 2, rows, lanes] = both.astype(bf16)
+        return carry
+
+    lax.fori_loop(0, TONES // 4, fold, 0)
+
+    def lags(pair, carry):
+        rows = pl.ds(pl.multiple_of(pair * 16, 16), 16)
+        base = constant[rows, :]
+
+        def turn(kind, first, count):
+            both = jnp.dot(lag_table[first * 8:(first + count) * 8, :], folded[kind, pair], preferred_element_type=f32)
+            both = both.reshape(count, 8, 256)
+            return jnp.concatenate([both[:, :, :128], both[:, :, 128:]], axis=1)
+
+        cosines, sines = turn(0, 0, 33) + base, turn(1, 33, 32)
+        out_ref[64, rows, :] = cosines[0].astype(bf16)
+        for lag in range(1, 33):
+            if lag < 32:
+                out_ref[64 + 2 * lag, rows, :] = (cosines[lag] - sines[lag - 1]).astype(bf16)
+            out_ref[64 - 2 * lag, rows, :] = (cosines[lag] + sines[lag - 1]).astype(bf16)
+        cosines, sines = turn(2, 65, 32) + base, turn(3, 97, 32)
+        for lag in range(32):
+            out_ref[65 + 2 * lag, rows, :] = (cosines[lag] - sines[lag]).astype(bf16)
+            out_ref[63 - 2 * lag, rows, :] = (cosines[lag] + sines[lag]).astype(bf16)
+        return carry
+
+    lax.fori_loop(0, CHANNELS // 16, lags, 0)
+
+
+def correlate(left_near, left_far, right_near, right_far):
+    tables = [jnp.asarray(table, jnp.bfloat16) for table in (*window_tables(), lag_tables())]
+    vmem = pl.BlockSpec(memory_space=pltpu.VMEM)
+    bf16 = jnp.bfloat16
+    return pl.pallas_call(
+        correlate_kernel,
+        out_shape=jax.ShapeDtypeStruct((LAGS, CHANNELS, CHANNELS), bf16),
+        in_specs=[vmem] * 7,
+        out_specs=vmem,
+        scratch_shapes=[
+            pltpu.VMEM((2 * BINS, SEGMENTS * CHANNELS), bf16),
+            pltpu.VMEM((2 * BINS, SEGMENTS * CHANNELS), bf16),
+            pltpu.VMEM((TONES, SEGMENTS * 16, CHANNELS), bf16),
+            pltpu.VMEM((TONES, SEGMENTS * 16, 2 * CHANNELS), bf16),
+            pltpu.VMEM((4, CHANNELS // 16, TONES // 2 * 8, 256), bf16),
+            pltpu.VMEM((CHANNELS, CHANNELS), jnp.float32),
+        ],
+        compiler_params=pltpu.CompilerParams(vmem_limit_bytes=56 * 2**20),
+    )(*tables, left_near, left_far, right_near, right_far)
 
 
 def swapped(value, bit):
@@ -190,19 +299,15 @@
 
 def per_device(spectra, plan):
     mine = spectra[0]
-    seg_dev, bin_count = mine.shape[0], mine.shape[3]
-    table_matrix = lag_table(bin_count, LAGS)
-    group_count = lax.axis_size("seg")
-    factor = 1.0 / math.sqrt(2.0 * seg_dev * group_count * bin_count)
     entry = lax.dynamic_index_in_dim(plan[:, 0], lax.axis_index("seg"), keepdims=False)
     mask = jnp.bitwise_xor(entry, lax.axis_index("ch"))
     others = lax.ppermute(mine, "seg", [(0, 1), (1, 0)])
-    left = jnp.concatenate([mine, others], axis=0)
-    moved = jnp.where(mask & 16 == 16, swapped(left, 16), left)
+    moved = jnp.concatenate([mine, others], axis=0)
+    moved = jnp.where(mask & 16 == 16, swapped(moved, 16), moved)
     moved = jnp.where(mask & 1 == 1, swapped(moved, 1), moved)
-    right = ring_move(plan, moved[:seg_dev], moved[seg_dev:]).reshape(left.shape)
-    lags_now = correlate(left, right, table_matrix)
-    return (lags_now * factor).astype(jnp.bfloat16)[None, None]
+    right = ring_move(plan, moved[:3], moved[3:])
+    near, far = mine.reshape(ROWS, BINS), others.reshape(ROWS, BINS)
+    return correlate(near, far, right[0], right[1])[None, None]
 
 
 def solution(mesh):

time: 327 us -> 205 us (0.63)
  local copies, waits for them, and re-layouts: 49.1 us -> 2.62 us
  matrix products: 39.6 us -> 0 us
  other arithmetic: 24.7 us -> 1.97 us
  Pallas kernels: 148 us -> 133 us
    pallas_call x1, Pallas kernels: 148 us -> 105 us  [ring_move(): pl.pallas_call(ring_kernel, out_shape=jax.ShapeDtypeStruct((2, ROWS, widt...]
    dot_general x16 -> x0, matrix products: 39.6 us -> none  [the longest x8 24.6 us: one_slab(): jnp.einsum('sif,sjf->fij', left_both, right_both, preferred_element_type=...]
    pallas_call x0 -> x1, Pallas kernels: none -> 27.1 us  [correlate(): pl.pallas_call(correlate_kernel, out_shape=jax.ShapeDtypeStruct((LAGS, CH...]
    concatenate x8 -> x0, local copies, waits for them, and re-layouts: 15.8 us -> none  [one_slab(): left_both = jnp.concatenate([plain_rows, turned_rows], axis=1)]
    dynamic_update_slice x16 -> x0, local copies, waits for them, and re-layouts: 13.1 us -> none  [one_slab(): return lax.dynamic_update_slice_in_dim(collected, lag_part, first, 1)]
    neg x8 -> x0, other arithmetic: 7.29 us -> none  [one_slab(): turned_rows = jnp.concatenate([row_slab[:, 1], -row_slab[:, 0]], axis=0)]
    broadcast_in_dim x1 -> x0, other arithmetic: 6.64 us -> none  [per_device(): return (lags_now * factor).astype(jnp.bfloat16)[None, None]]
    concatenate x19 -> x1, other arithmetic: 7.72 us -> 1.55 us  [per_device(): moved = jnp.concatenate([mine, others], axis=0)]
  transfers between devices with their start and end apart: 3 -> 3, of which waited for: 3 -> 3; matrix products, arithmetic and copies ran while one was open for 1% -> 0% of each run, Pallas kernels for 0% -> 0%
where the time goes in v2:
time: 205 us; the launch traced here: 202 us
  Pallas kernels  133 us (65%)
  waiting for transfers between devices  56.2 us (27%)
  starting transfers between devices  8.09 us (4%)
  local copies, waits for them, and re-layouts  2.62 us (1%)
    pallas_call x1, Pallas kernels, ring_move(): pl.pallas_call(ring_kernel, out_shape=jax.ShapeDtypeStruct((2, ROWS, widt...  105 us
    ppermute x2, waiting for transfers between devices, swapped(): lax.ppermute(value, 'ch', [(block, block ^ bit) for block in range(lax.ax...  36.7 us
    pallas_call x1, Pallas kernels, correlate(): pl.pallas_call(correlate_kernel, out_shape=jax.ShapeDtypeStruct((LAGS, CH...  27.1 us
    ppermute x1, waiting for transfers between devices, per_device(): others = lax.ppermute(mine, 'seg', [(0, 1), (1, 0)])  19.6 us
    ppermute x2, starting transfers between devices, swapped(): lax.ppermute(value, 'ch', [(block, block ^ bit) for block in range(lax.ax...  4.66 us
  transfers between devices with their start and end apart: 3, of which 3 were waited for; matrix products, arithmetic and copies ran while one was open for 0% of the time, Pallas kernels for 0%

profile of v2, /device:TPU:6, one launch (start us, length us, event | category | flops | bytes accessed | tf_op | source)
XLA Modules:
  0.0 202.2 jit_solution(3357436196830600978)
XLA Ops:
  0.0 0.0 copy-start.3
  0.0 0.0 copy-start.1
  0.0 3.4 %collective-permute-start = (bf16[3,2,128,512]{3,2,1,0:T(8,128)(2,1)}, bf16[3,2,128,512]{3,2,1,0:T(8,128)(2,1)S(1)}, u32[]{:S(2)}, u32[]{:S(2)}) collective-permute-start(bf16[3,2,128,512]{3,2,1,0:T(8,128)(2,1)} %bitcast.13), channel_id=1, source_target_pairs={{0,1},{1,0},{2,3},{3,2},{4,5},{5,4},{6,7},{7,6},{8,9},{9,8},{10,11... | collective-permute-start | bytes 2359304 | tf_op jit(solution)/shard_map/ppermute | solution.py:304
  3.4 19.6 %collective-permute-done = bf16[3,2,128,512]{3,2,1,0:T(8,128)(2,1)S(1)} collective-permute-done((bf16[3,2,128,512]{3,2,1,0:T(8,128)(2,1)}, bf16[3,2,128,512]{3,2,1,0:T(8,128)(2,1)S(1)}, u32[]{:S(2)}, u32[]{:S(2)}) %collective-permute-start) | collective-permute-done | bytes 786464 | tf_op jit(solution)/shard_map/ppermute | solution.py:304
  23.0 0.0 copy-start.2
  23.0 1.6 pad_maximum_fusion
  24.6 2.7 %collective-permute-start.1 = (bf16[6,2,128,512]{3,2,1,0:T(8,128)(2,1)S(1)}, bf16[6,2,128,512]{3,2,1,0:T(8,128)(2,1)}, u32[]{:S(2)}, u32[]{:S(2)}) collective-permute-start(bf16[6,2,128,512]{3,2,1,0:T(8,128)(2,1)S(1)} %pad_maximum_fusion), channel_id=1, source_target_pairs={{0,32},{2,34},{4,36},{6,38},{8,40},{10,42},{12,44},{14,46},{16,48}... | collective-permute-start | bytes 4718600 | tf_op jit(solution)/shard_map/ppermute | solution.py:297
  27.3 0.0 copy-done.3
  27.3 0.6 constant_dynamic-slice_fusion
  28.6 33.3 %collective-permute-done.1 = bf16[6,2,128,512]{3,2,1,0:T(8,128)(2,1)} collective-permute-done((bf16[6,2,128,512]{3,2,1,0:T(8,128)(2,1)S(1)}, bf16[6,2,128,512]{3,2,1,0:T(8,128)(2,1)}, u32[]{:S(2)}, u32[]{:S(2)}) %collective-permute-start.1) | collective-permute-done | bytes 1572896 | tf_op jit(solution)/shard_map/ppermute | solution.py:297
  61.8 0.0 copy-done.2
  61.8 0.0 copy-done.1
  61.8 0.2 broadcast_select_fusion
  62.1 1.9 collective-permute-start.2
  64.0 0.1 copy.7.plan_ref
  64.1 3.4 %collective-permute-done.2 = bf16[6,2,128,512]{3,2,1,0:T(8,128)(2,1)} collective-permute-done((bf16[6,2,128,512]{3,2,1,0:T(8,128)(2,1)S(1)}, bf16[6,2,128,512]{3,2,1,0:T(8,128)(2,1)}, u32[]{:S(2)}, u32[]{:S(2)}) %collective-permute-start.2) | collective-permute-done | bytes 1572896 | tf_op jit(solution)/shard_map/ppermute | solution.py:297
  67.5 0.2 broadcast_select_fusion.1
  67.7 0.0 copy-start
  67.7 0.1 fusion
  67.8 0.6 copy-done
  68.4 105.4 %shard_map.64 = bf16[2,768,512]{2,1,0:T(8,128)(2,1)S(1)} custom-call(s32[2,1]{1,0:T(2,128)S(1)} %copy.7.plan_ref, s32[1024]{0:T(1024)S(1)} %copy-done, bf16[768,512]{1,0:T(8,128)(2,1)S(1)} %bitcast.12, bf16[768,512]{1,0:T(8,128)(2,1)S(1)} %bitcast.11), custom_call_target="tpu_custom_call" | custom-call | tf_op jit(solution)/shard_map/pallas_call | solution.py:133
  173.8 1.3 slice_bitcast_fusion
  175.0 27.1 %shard_map.65 = bf16[128,128,128]{2,1,0:T(8,128)(2,1)} custom-call(bf16[2048,1024]{1,0:T(8,128)(2,1)} %constant.28.clone.left_table, bf16[2048,1024]{1,0:T(8,128)(2,1)} %constant.29.clone.right_table, bf16[1032,512]{1,0:T(8,128)(2,1)} %constant.30.clone.lag_table, bf16[768,512]{1,0:T(8,128)(2,1)} %bitcast.15, bf16[768,512]{1,0:T(8,128)(2,1)} %bitcast.17, ...), custom_call_target="tpu_custom_call" | custom-call | tf_op jit(solution)/shard_map/pallas_call | solution.py:279
Async XLA Ops:
  0.0 27.3 %copy-start.3 = (s32[2,1]{0,1:T(1,128)S(1)}, s32[2,1]{0,1:T(1,128)}, u32[]{:S(2)}) copy-start(s32[2,1]{0,1:T(1,128)} %param.7) | copy-start | bytes 28
  0.0 61.8 %copy-start.1 = (bf16[1,3,2,128,512]{4,3,2,1,0:T(8,128)(2,1)S(1)}, bf16[1,3,2,128,512]{4,3,2,1,0:T(8,128)(2,1)}, u32[]{:S(2)}) copy-start(bf16[1,3,2,128,512]{4,3,2,1,0:T(8,128)(2,1)} %param.6) | copy-start | bytes 2359300
  0.0 23.0 %collective-permute-start = (bf16[3,2,128,512]{3,2,1,0:T(8,128)(2,1)}, bf16[3,2,128,512]{3,2,1,0:T(8,128)(2,1)S(1)}, u32[]{:S(2)}, u32[]{:S(2)}) collective-permute-start(bf16[3,2,128,512]{3,2,1,0:T(8,128)(2,1)} %bitcast.13), channel_id=1, source_target_pairs={{0,1},{1,0},{2,3},{3,2},{4,5},{5,4},{6,7},{7,6},{8,9},{9,8},{10,11... | collective-permute-start | bytes 2359304 | tf_op jit(solution)/shard_map/ppermute | solution.py:304
  23.0 38.8 %copy-start.2 = (bf16[3,2,128,512]{3,2,1,0:T(8,128)(2,1)}, bf16[3,2,128,512]{3,2,1,0:T(8,128)(2,1)S(1)}, u32[]{:S(2)}) copy-start(bf16[3,2,128,512]{3,2,1,0:T(8,128)(2,1)S(1)} %collective-permute-done) | copy-start | bytes 2359300
  24.6 37.3 %collective-permute-start.1 = (bf16[6,2,128,512]{3,2,1,0:T(8,128)(2,1)S(1)}, bf16[6,2,128,512]{3,2,1,0:T(8,128)(2,1)}, u32[]{:S(2)}, u32[]{:S(2)}) collective-permute-start(bf16[6,2,128,512]{3,2,1,0:T(8,128)(2,1)S(1)} %pad_maximum_fusion), channel_id=1, source_target_pairs={{0,32},{2,34},{4,36},{6,38},{8,40},{10,42},{12,44},{14,46},{16,48}... | collective-permute-start | bytes 4718600 | tf_op jit(solution)/shard_map/ppermute | solution.py:297
  62.1 5.4 %collective-permute-start.2 = (bf16[6,2,128,512]{3,2,1,0:T(8,128)(2,1)S(1)}, bf16[6,2,128,512]{3,2,1,0:T(8,128)(2,1)}, u32[]{:S(2)}, u32[]{:S(2)}) collective-permute-start(bf16[6,2,128,512]{3,2,1,0:T(8,128)(2,1)S(1)} %broadcast_select_fusion), channel_id=1, source_target_pairs={{0,2},{2,0},{4,6},{6,4},{8,10},{10,8},{12,14},{14,12},{16,18},{18,... | collective-permute-start | bytes 4718600 | tf_op jit(solution)/shard_map/ppermute | solution.py:297
  67.7 0.7 copy-start

commit v3 on v2

--- a/solution.py
+++ b/solution.py
@@ -16,7 +16,8 @@
 SLOTS = 2 * CHUNKS + 2
 STREAMS = 4
 ROWS = 768
-PIECE = ROWS // (STREAMS * CHUNKS)
+BLOCK = ROWS // CHUNKS
+PIECE = BLOCK // STREAMS
 
 
 def path(mask, place):
@@ -42,30 +43,94 @@
     return table.reshape(-1)
 
 
-def ring_kernel(plan_ref, table_ref, near_ref, far_ref, out_ref, middle, landed, staged, send_sem, recv_sem):
+def ring_kernel(plan_ref, table_ref, mine_ref, others_ref, near_out, far_out, first, middle, beside, across, opposite,
+                chosen, swapped, landed, staged, send_sem, recv_sem, x_send, x_recv):
     ch, seg = lax.axis_index("ch"), lax.axis_index("seg")
     z, y = ch // 2 % RING, ch // 32
+    turned = ch + 16 - ch // 16 % 2 * 32
     targets = [
-        (ch + 32) % 256,
-        (ch + 224) % 256,
-        ch - z * 2 + (z + 1) % RING * 2,
-        ch - z * 2 + (z + RING - 1) % RING * 2,
+        ((ch + 32) % 256, seg),
+        ((ch + 224) % 256, seg),
+        (ch - z * 2 + (z + 1) % RING * 2, seg),
+        (ch - z * 2 + (z + RING - 1) % RING * 2, seg),
+        (turned, seg),
+        (turned, 1 - seg),
+        (ch + 1 - ch % 2 * 2, seg),
     ]
     mask = plan_ref[seg, 0] ^ ch
     bases = [(((mask // 32) % RING) * RING + y) * 16, (((mask // 2) % RING) * RING + z) * 16]
+    x_bit, core_bit = mask // 16 % 2, mask % 2
 
     barrier = pltpu.get_barrier_semaphore()
     for target in targets:
-        pl.semaphore_signal(barrier, inc=1, device_id=(target, seg), device_id_type=MESH)
-    pl.semaphore_wait(barrier, 4)
-
-    halves = (near_ref, far_ref)
+        pl.semaphore_signal(barrier, inc=1, device_id=target, device_id_type=MESH)
+    pl.semaphore_wait(barrier, len(targets))
+
+    def rows(start, count):
+        return pl.ds(pl.multiple_of(start, 16), count)
+
+    def x_copy(kind, chunk):
+        all_rows = rows(chunk * BLOCK, BLOCK)
+        upper, lower = rows(chunk * BLOCK, BLOCK // 2), rows(chunk * BLOCK + BLOCK // 2, BLOCK // 2)
+        source, goal, target = [
+            (mine_ref.at[all_rows, :], beside.at[all_rows, :], targets[4]),
+            (mine_ref.at[all_rows, :], across.at[all_rows, :], targets[5]),
+            (beside.at[upper, :], opposite.at[upper, :], targets[5]),
+            (across.at[lower, :], opposite.at[lower, :], targets[4]),
+            (chosen.at[0, all_rows, :], swapped.at[0, all_rows, :], targets[6]),
+            (chosen.at[1, all_rows, :], swapped.at[1, all_rows, :], targets[6]),
+        ][kind]
+        return pltpu.make_async_remote_copy(
+            src_ref=source,
+            dst_ref=goal,
+            send_sem=x_send.at[kind, chunk],
+            recv_sem=x_recv.at[kind, chunk],
+            device_id=target,
+            device_id_type=MESH,
+        )
+
+    def spread(chunk):
+        for kind in (0, 1):
+            x_copy(kind, chunk).start()
+
+    def forward(chunk):
+        for kind in (0, 1):
+            x_copy(kind, chunk).wait_recv()
+        for kind in (2, 3):
+            x_copy(kind, chunk).start()
+
+    def choose(chunk):
+        for kind in (2, 3):
+            x_copy(kind, chunk).wait_recv()
+        here = rows(chunk * BLOCK, BLOCK)
+        others_ref[here, :] = opposite[here, :]
+        chosen[0, here, :] = jnp.where(x_bit == 1, beside[here, :], mine_ref[here, :])
+        chosen[1, here, :] = jnp.where(x_bit == 1, across[here, :], opposite[here, :])
+        for kind in (4, 5):
+            x_copy(kind, chunk).start()
+
+    def settle(chunk):
+        here = rows(chunk * BLOCK, BLOCK)
+        for half in range(2):
+            x_copy(4 + half, chunk).wait_recv()
+            first[half, here, :] = jnp.where(core_bit == 1, swapped[half, here, :], chosen[half, here, :])
+
+    def finish(chunk):
+        for kind in range(6):
+            x_copy(kind, chunk).wait_send()
+
+    spread(0)
+    forward(0)
+    spread(1)
+    choose(0)
+    settle(0)
+
     for stage in range(2):
-        source = halves if stage == 0 else (middle.at[0], middle.at[1])
-        goal = (middle.at[0], middle.at[1]) if stage == 0 else (out_ref.at[0], out_ref.at[1])
-
-        def rows(stream, chunk):
-            return pl.ds(pl.multiple_of(stream * (ROWS // STREAMS) + chunk * PIECE, 16), PIECE)
+        source = (first.at[0], first.at[1]) if stage == 0 else (middle.at[0], middle.at[1])
+        goal = (middle.at[0], middle.at[1]) if stage == 0 else (near_out, far_out)
+
+        def piece(stream, chunk):
+            return rows(chunk * BLOCK + stream * PIECE, PIECE)
 
         def copy(link, stream, slot, stage=stage):
             return pltpu.make_async_remote_copy(
@@ -73,7 +138,7 @@
                 dst_ref=landed.at[stage, link, stream, slot],
                 send_sem=send_sem.at[link, stream, slot % 2],
                 recv_sem=recv_sem.at[stage, link, stream, slot],
-                device_id=(targets[link], seg),
+                device_id=targets[link],
                 device_id_type=MESH,
             )
 
@@ -81,7 +146,7 @@
             for stream in range(STREAMS):
                 for dim in range(2):
                     chunk = jnp.minimum(slot // 2, CHUNKS - 1)
-                    own = source[dim ^ stage][rows(stream, chunk), :]
+                    own = source[dim ^ stage][piece(stream, chunk), :]
                     for direction in range(2):
                         link = 2 * dim + direction
                         value = own
@@ -98,23 +163,49 @@
             for dim in range(2):
                 code = table_ref[bases[dim] + 8 + chunk % 2]
                 for stream in range(STREAMS):
-                    value = source[dim ^ stage][rows(stream, chunk), :]
+                    value = source[dim ^ stage][piece(stream, chunk), :]
                     for place in range(8):
                         found = landed[stage, 2 * dim + place // 4, stream, 2 * chunk + place % 4]
                         value = jnp.where(code == place, found, value)
-                    goal[dim ^ stage][rows(stream, chunk), :] = value
+                    goal[dim ^ stage][piece(stream, chunk), :] = value
 
         send(0, first=True)
+        if stage == 0:
+            forward(1)
         send(1, second=True)
-
-        def pair(number, carry, send=send, pick=pick):
+        if stage == 0:
+            choose(1)
+            spread(2)
+
+        def pair(number, carry, stage=stage, send=send, pick=pick):
+            if stage == 0:
+
+                @pl.when(number < CHUNKS)
+                def _():
+                    settle(number)
+
             send(2 * number)
+            if stage == 0:
+
+                @pl.when(number < CHUNKS - 1)
+                def _():
+                    forward(number + 1)
 
             @pl.when(number >= 2)
             def _():
                 pick(number - 2)
 
             send(2 * number + 1)
+            if stage == 0:
+
+                @pl.when(number < CHUNKS - 1)
+                def _():
+                    choose(number + 1)
+
+                @pl.when(number < CHUNKS - 2)
+                def _():
+                    spread(number + 2)
+
             return carry
 
         lax.fori_loop(1, SLOTS // 2, pair, 0)
@@ -125,27 +216,39 @@
                 copy(link, stream, SLOTS - 1).wait_send()
         pick(CHUNKS - 1)
 
-
-def ring_move(plan, near, far):
-    width = near.shape[-1]
+    for chunk in range(CHUNKS):
+        finish(chunk)
+
+
+def ring_move(plan, mine):
+    width = mine.shape[-1]
     vmem = pl.BlockSpec(memory_space=pltpu.VMEM)
     smem = pl.BlockSpec(memory_space=pltpu.SMEM)
+    bf16 = jnp.bfloat16
     return pl.pallas_call(
         ring_kernel,
-        out_shape=jax.ShapeDtypeStruct((2, ROWS, width), jnp.bfloat16),
-        in_specs=[smem, smem, vmem, vmem],
-        out_specs=vmem,
+        out_shape=[jax.ShapeDtypeStruct((ROWS, width), bf16)] * 3,
+        in_specs=[smem, smem, vmem],
+        out_specs=[vmem] * 3,
         scratch_shapes=[
-            pltpu.VMEM((2, ROWS, width), jnp.bfloat16),
-            pltpu.VMEM((2, 4, STREAMS, SLOTS, PIECE, width), jnp.bfloat16),
-            pltpu.VMEM((4, STREAMS, 2, PIECE, width), jnp.bfloat16),
+            pltpu.VMEM((2, ROWS, width), bf16),
+            pltpu.VMEM((2, ROWS, width), bf16),
+            pltpu.VMEM((ROWS, width), bf16),
+            pltpu.VMEM((ROWS, width), bf16),
+            pltpu.VMEM((ROWS, width), bf16),
+            pltpu.VMEM((2, ROWS, width), bf16),
+            pltpu.VMEM((2, ROWS, width), bf16),
+            pltpu.VMEM((2, 4, STREAMS, SLOTS, PIECE, width), bf16),
+            pltpu.VMEM((4, STREAMS, 2, PIECE, width), bf16),
             pltpu.SemaphoreType.DMA((4, STREAMS, 2)),
             pltpu.SemaphoreType.DMA((2, 4, STREAMS, SLOTS)),
+            pltpu.SemaphoreType.DMA((6, CHUNKS)),
+            pltpu.SemaphoreType.DMA((6, CHUNKS)),
         ],
         compiler_params=pltpu.CompilerParams(
             collective_id=0, has_side_effects=True, vmem_limit_bytes=48 * 2**20
         ),
-    )(plan, jnp.asarray(ring_table()), near.reshape(ROWS, width), far.reshape(ROWS, width))
+    )(plan, jnp.asarray(ring_table()), mine)
 
 
 BINS = 512
@@ -293,21 +396,10 @@
     )(*tables, left_near, left_far, right_near, right_far)
 
 
-def swapped(value, bit):
-    return lax.ppermute(value, "ch", [(block, block ^ bit) for block in range(lax.axis_size("ch"))])
-
-
 def per_device(spectra, plan):
-    mine = spectra[0]
-    entry = lax.dynamic_index_in_dim(plan[:, 0], lax.axis_index("seg"), keepdims=False)
-    mask = jnp.bitwise_xor(entry, lax.axis_index("ch"))
-    others = lax.ppermute(mine, "seg", [(0, 1), (1, 0)])
-    moved = jnp.concatenate([mine, others], axis=0)
-    moved = jnp.where(mask & 16 == 16, swapped(moved, 16), moved)
-    moved = jnp.where(mask & 1 == 1, swapped(moved, 1), moved)
-    right = ring_move(plan, moved[:3], moved[3:])
-    near, far = mine.reshape(ROWS, BINS), others.reshape(ROWS, BINS)
-    return correlate(near, far, right[0], right[1])[None, None]
+    mine = spectra.reshape(ROWS, BINS)
+    others, near, far = ring_move(plan, mine)
+    return correlate(mine, others, near, far)[None, None]
 
 
 def solution(mesh):

time: 205 us -> 157 us (0.77)
  waiting for transfers between devices: 56.2 us -> 0 us
  Pallas kernels: 133 us -> 150 us
  starting transfers between devices: 8.09 us -> 0 us
  local copies, waits for them, and re-layouts: 2.62 us -> 5.24 us
    ppermute x3 -> x0, waiting for transfers between devices: 56.2 us -> none  [the longest x2 36.7 us: swapped(): lax.ppermute(value, 'ch', [(block, block ^ bit) for block in range(lax.ax...]
    pallas_call x1, Pallas kernels: 105 us -> 123 us  [ring_move(): pl.pallas_call(ring_kernel, out_shape=[jax.ShapeDtypeStruct((ROWS, width)...]
    ppermute x3 -> x0, starting transfers between devices: 8.09 us -> none  [the longest x2 4.66 us: swapped(): lax.ppermute(value, 'ch', [(block, block ^ bit) for block in range(lax.ax...]
    unnamed x9 -> x11, local copies, waits for them, and re-layouts: 0.68 us -> 5.24 us
  transfers between devices with their start and end apart: 3 -> 0, of which waited for: 3 -> 0; matrix products, arithmetic and copies ran while one was open for 0% -> 0% of each run, Pallas kernels for 0% -> 0%
where the time goes in v3:
time: 157 us; the launch traced here: 155 us
  Pallas kernels  150 us (96%)
  local copies, waits for them, and re-layouts  5.24 us (3%)
    pallas_call x1, Pallas kernels, ring_move(): pl.pallas_call(ring_kernel, out_shape=[jax.ShapeDtypeStruct((ROWS, width)...  123 us
    pallas_call x1, Pallas kernels, correlate(): pl.pallas_call(correlate_kernel, out_shape=jax.ShapeDtypeStruct((LAGS, CH...  27.1 us
    unnamed x11, local copies, waits for them, and re-layouts  5.24 us

profile of v3, /device:TPU:6, one launch (start us, length us, event | category | flops | bytes accessed | tf_op | source)
XLA Modules:
  0.0 155.2 jit_solution(14759407412528544641)
XLA Ops:
  0.0 0.7 copy.7.plan_ref
  0.7 0.0 copy-start
  0.7 1.1 copy-done
  1.9 0.0 copy-start.4
  1.9 0.7 copy-done.4
  2.6 122.8 %shard_map.64 = (bf16[768,512]{1,0:T(8,128)(2,1)S(1)}, bf16[768,512]{1,0:T(8,128)(2,1)S(1)}, bf16[768,512]{1,0:T(8,128)(2,1)S(1)}) custom-call(s32[2,1]{1,0:T(2,128)S(1)} %copy.7.plan_ref, s32[1024]{0:T(1024)S(1)} %copy-done.4, bf16[768,512]{1,0:T(8,128)(2,1)S(1)} %bitcast.3), custom_call_target="tpu_custom_call" | custom-call | tf_op jit(solution)/shard_map/pallas_call | solution.py:228
  125.4 0.0 copy-start.1
  125.4 0.9 copy-done.1
  126.3 0.0 copy-start.2
  126.3 0.9 copy-done.2
  127.2 0.0 copy-start.3
  127.2 0.9 copy-done.3
  128.1 27.1 %shard_map.65 = bf16[128,128,128]{2,1,0:T(8,128)(2,1)} custom-call(bf16[2048,1024]{1,0:T(8,128)(2,1)} %constant.9.clone.left_table, bf16[2048,1024]{1,0:T(8,128)(2,1)} %constant.10.clone.right_table, bf16[1032,512]{1,0:T(8,128)(2,1)} %constant.11.clone.lag_table, bf16[768,512]{1,0:T(8,128)(2,1)} %bitcast.2, bf16[768,512]{1,0:T(8,128)(2,1)} %copy-done.1, ...), custom_call_target="tpu_custom_call" | custom-call | tf_op jit(solution)/shard_map/pallas_call | solution.py:382
Async XLA Ops:
  0.7 1.1 copy-start
  1.9 0.7 copy-start.4
  125.4 0.9 copy-start.1
  126.3 0.9 copy-start.2
  127.2 0.9 copy-start.3

commit v4 on v3

--- a/solution.py
+++ b/solution.py
@@ -41,10 +41,33 @@
                 back, hops, start = path(mask, place ^ mask)
                 row[8:10] = back * 4 + start + hops - 1
     return table.reshape(-1)
-
-
-def ring_kernel(plan_ref, table_ref, mine_ref, others_ref, near_out, far_out, first, middle, beside, across, opposite,
-                chosen, swapped, landed, staged, send_sem, recv_sem, x_send, x_recv):
+BINS = 512
+SEGMENTS = 6
+CHANNELS = 128
+WINDOWS = 8
+TONES = 128
+SPAN = 2 * TONES
+STEP = 256
+PARTS = TONES * 16 // STEP
+
+
+def sixth(near, far, segment, part):
+    first = (segment % 3) * 2 * CHANNELS + part * CHANNELS
+    return (near if segment < 3 else far)[first:first + CHANNELS, :]
+
+
+def lay_out(near, far, turned, segments):
+    for segment in segments:
+        lanes = slice(segment * CHANNELS, (segment + 1) * CHANNELS)
+        for part in range(2):
+            turned[part * BINS:(part + 1) * BINS, lanes] = sixth(near, far, segment, part).T
+
+
+def ring_kernel(plan_ref, table_ref, left_table, mine_ref, tones_out, flat_out, near_out, far_out, first, middle, beside, across,
+                opposite, chosen, swapped, landed, staged, left_rows, left_turned, left_tones, flat, send_sem, recv_sem, x_send,
+                x_recv, load_sem, store_sem):
+    load = pltpu.make_async_copy(left_table, left_rows, load_sem)
+    load.start()
     ch, seg = lax.axis_index("ch"), lax.axis_index("seg")
     z, y = ch // 2 % RING, ch // 32
     turned = ch + 16 - ch // 16 % 2 * 32
@@ -103,7 +126,6 @@
         for kind in (2, 3):
             x_copy(kind, chunk).wait_recv()
         here = rows(chunk * BLOCK, BLOCK)
-        others_ref[here, :] = opposite[here, :]
         chosen[0, here, :] = jnp.where(x_bit == 1, beside[here, :], mine_ref[here, :])
         chosen[1, here, :] = jnp.where(x_bit == 1, across[here, :], opposite[here, :])
         for kind in (4, 5):
@@ -118,6 +140,26 @@
     def finish(chunk):
         for kind in range(6):
             x_copy(kind, chunk).wait_send()
+
+    def store(number):
+        where = pl.ds(number * (STEP // 16), STEP // 16)
+        return pltpu.make_async_copy(left_tones.at[where], tones_out.at[where], store_sem.at[number])
+
+    def left_part(number):
+        part = rows(number * STEP, STEP)
+        tones = jnp.dot(left_rows[part, :], left_turned[...], preferred_element_type=jnp.float32)
+        for segment in range(SEGMENTS):
+            piece_tones = tones[:, segment * CHANNELS:(segment + 1) * CHANNELS].reshape(STEP // 16, 16, CHANNELS)
+            depth = slice(segment * 16, (segment + 1) * 16)
+            left_tones[pl.ds(number * (STEP // 16), STEP // 16), depth, :] = piece_tones.astype(jnp.bfloat16)
+        store(number).start()
+
+    def flatten():
+        first_lane = lax.broadcasted_iota(jnp.int32, (CHANNELS, 128), 1) == 0
+        for segment in range(SEGMENTS):
+            value = sixth(mine_ref, opposite, segment, 1)[:, :128].astype(jnp.float32)
+            flat[segment * CHANNELS:(segment + 1) * CHANNELS, :] = jnp.where(first_lane, value, 0.0).astype(jnp.bfloat16)
+        pltpu.make_async_copy(flat, flat_out, store_sem.at[PARTS]).start()
 
     spread(0)
     forward(0)
@@ -172,10 +214,16 @@
         send(0, first=True)
         if stage == 0:
             forward(1)
+        else:
+            lay_out(mine_ref, opposite, left_turned, range(3))
         send(1, second=True)
         if stage == 0:
             choose(1)
             spread(2)
+        else:
+            lay_out(mine_ref, opposite, left_turned, range(3, 6))
+            flatten()
+            load.wait()
 
         def pair(number, carry, stage=stage, send=send, pick=pick):
             if stage == 0:
@@ -191,6 +239,9 @@
                 def _():
                     forward(number + 1)
 
+            else:
+                left_part(2 * number - 2)
+
             @pl.when(number >= 2)
             def _():
                 pick(number - 2)
@@ -205,6 +256,9 @@
                 @pl.when(number < CHUNKS - 2)
                 def _():
                     spread(number + 2)
+
+            else:
+                left_part(2 * number - 1)
 
             return carry
 
@@ -218,18 +272,27 @@
 
     for chunk in range(CHUNKS):
         finish(chunk)
-
-
-def ring_move(plan, mine):
+    for number in range(PARTS):
+        store(number).wait()
+    pltpu.make_async_copy(flat, flat_out, store_sem.at[PARTS]).wait()
+
+
+def ring_move(plan, mine, left_table):
     width = mine.shape[-1]
     vmem = pl.BlockSpec(memory_space=pltpu.VMEM)
     smem = pl.BlockSpec(memory_space=pltpu.SMEM)
+    hbm = pl.BlockSpec(memory_space=pl.ANY)
     bf16 = jnp.bfloat16
     return pl.pallas_call(
         ring_kernel,
-        out_shape=[jax.ShapeDtypeStruct((ROWS, width), bf16)] * 3,
-        in_specs=[smem, smem, vmem],
-        out_specs=[vmem] * 3,
+        out_shape=[
+            jax.ShapeDtypeStruct((TONES, SEGMENTS * 16, CHANNELS), bf16),
+            jax.ShapeDtypeStruct((SEGMENTS * CHANNELS, 128), bf16),
+            jax.ShapeDtypeStruct((ROWS, width), bf16),
+            jax.ShapeDtypeStruct((ROWS, width), bf16),
+        ],
+        in_specs=[smem, smem, hbm, vmem],
+        out_specs=[hbm, hbm, vmem, vmem],
         scratch_shapes=[
             pltpu.VMEM((2, ROWS, width), bf16),
             pltpu.VMEM((2, ROWS, width), bf16),
@@ -240,23 +303,21 @@
             pltpu.VMEM((2, ROWS, width), bf16),
             pltpu.VMEM((2, 4, STREAMS, SLOTS, PIECE, width), bf16),
             pltpu.VMEM((4, STREAMS, 2, PIECE, width), bf16),
+            pltpu.VMEM((TONES * 16, 2 * BINS), bf16),
+            pltpu.VMEM((2 * BINS, SEGMENTS * CHANNELS), bf16),
+            pltpu.VMEM((TONES, SEGMENTS * 16, CHANNELS), bf16),
+            pltpu.VMEM((SEGMENTS * CHANNELS, 128), bf16),
             pltpu.SemaphoreType.DMA((4, STREAMS, 2)),
             pltpu.SemaphoreType.DMA((2, 4, STREAMS, SLOTS)),
             pltpu.SemaphoreType.DMA((6, CHUNKS)),
             pltpu.SemaphoreType.DMA((6, CHUNKS)),
+            pltpu.SemaphoreType.DMA,
+            pltpu.SemaphoreType.DMA((PARTS + 1,)),
         ],
         compiler_params=pltpu.CompilerParams(
-            collective_id=0, has_side_effects=True, vmem_limit_bytes=48 * 2**20
+            collective_id=0, has_side_effects=True, vmem_limit_bytes=56 * 2**20
         ),
-    )(plan, jnp.asarray(ring_table()), mine)
-
-
-BINS = 512
-SEGMENTS = 6
-CHANNELS = 128
-WINDOWS = 8
-TONES = 128
-SPAN = 2 * TONES
+    )(plan, jnp.asarray(ring_table()), left_table, mine)
 
 
 def window_tables():
@@ -287,48 +348,63 @@
     return np.kron(np.concatenate(parts, axis=0) * scale, np.eye(8))
 
 
-def correlate_kernel(left_table, right_table, lag_table, left_near, left_far, right_near, right_far, out_ref,
-                     left_turned, right_turned, left_tones, right_tones, folded, constant):
+def correlate_kernel(right_table, lag_table, left_ref, flat_ref, near_ref, far_ref, out_ref,
+                     right_rows, lag_rows, left_tones, flat, near, far, right_turned, right_tones, folded, constant, held,
+                     load_sem, part_sem, out_sem):
     f32, bf16 = jnp.float32, jnp.bfloat16
-
-    def block(near, far, segment, part):
-        source = near if segment < 3 else far
-        first = (segment % 3) * 2 * CHANNELS + part * CHANNELS
-        return source[first:first + CHANNELS, :]
-
-    for segment in range(SEGMENTS):
-        lanes = slice(segment * CHANNELS, (segment + 1) * CHANNELS)
-        for part in range(2):
-            rows = slice(part * BINS, (part + 1) * BINS)
-            left_turned[rows, lanes] = block(left_near, left_far, segment, part).T
-            right_turned[rows, lanes] = block(right_near, right_far, segment, part).T
-
-    first_lane = lax.broadcasted_iota(jnp.int32, (CHANNELS, 128), 1) == 0
-    total = jnp.zeros((CHANNELS, CHANNELS), f32)
-    for segment in range(SEGMENTS):
-        mine = jnp.where(first_lane, block(left_near, left_far, segment, 1)[:, :128].astype(f32), 0.0).astype(bf16)
-        theirs = block(right_near, right_far, segment, 1)[:, :128]
-        total += lax.dot_general(mine, theirs, (((1,), (1,)), ((), ())), preferred_element_type=f32)
-    constant[...] = total * (1.0 / math.sqrt(2.0 * SEGMENTS * BINS))
-
-    step = 256
+    loads = [
+        pltpu.make_async_copy(source, goal, load_sem.at[number])
+        for number, (source, goal) in enumerate(
+            [(near_ref, near), (far_ref, far), (flat_ref, flat), (left_ref, left_tones), (lag_table, lag_rows)]
+        )
+    ]
+
+    def part_rows(number):
+        return pl.ds(pl.multiple_of(number * STEP, STEP), STEP)
+
+    def part_load(number):
+        rows = part_rows(number)
+        return pltpu.make_async_copy(right_table.at[rows, :], right_rows.at[rows, :], part_sem.at[number])
+
+    def result(pair):
+        rows = pl.ds(pl.multiple_of(pair * 16, 16), 16)
+        return pltpu.make_async_copy(held.at[pair % 2], out_ref.at[:, rows, :], out_sem.at[pair % 2])
+
+    for load in loads[:2]:
+        load.start()
+    for number in range(PARTS):
+        part_load(number).start()
+    for load in loads[2:]:
+        load.start()
+
+    loads[0].wait()
+    lay_out(near, far, right_turned, range(3))
+    loads[1].wait()
+    lay_out(near, far, right_turned, range(3, 6))
 
     def tones_of(number, carry):
-        rows = pl.ds(pl.multiple_of(number * step, step), step)
-        where = pl.ds(number * (step // 16), step // 16)
-        left = jnp.dot(left_table[rows, :], left_turned[...], preferred_element_type=f32)
-        right = jnp.dot(right_table[rows, :], right_turned[...], preferred_element_type=f32)
+        part_load(number).wait()
+        where = pl.ds(number * (STEP // 16), STEP // 16)
+        right = jnp.dot(right_rows[part_rows(number), :], right_turned[...], preferred_element_type=f32)
         for segment in range(SEGMENTS):
             lanes = slice(segment * CHANNELS, (segment + 1) * CHANNELS)
             depth = slice(segment * 16, (segment + 1) * 16)
-            left_tones[where, depth, :] = left[:, lanes].reshape(step // 16, 16, CHANNELS).astype(bf16)
-            plain = right[:, lanes].reshape(step // 16, 2, 8, CHANNELS)
-            right_tones[where, depth, :CHANNELS] = plain.reshape(step // 16, 16, CHANNELS).astype(bf16)
+            plain = right[:, lanes].reshape(STEP // 16, 2, 8, CHANNELS)
+            right_tones[where, depth, :CHANNELS] = plain.reshape(STEP // 16, 16, CHANNELS).astype(bf16)
             turned = jnp.concatenate([-plain[:, 1], plain[:, 0]], axis=1)
             right_tones[where, depth, CHANNELS:] = turned.astype(bf16)
         return carry
 
-    lax.fori_loop(0, TONES * 16 // step, tones_of, 0)
+    lax.fori_loop(0, PARTS, tones_of, 0)
+
+    loads[2].wait()
+    total = jnp.zeros((CHANNELS, CHANNELS), f32)
+    for segment in range(SEGMENTS):
+        mine = flat[segment * CHANNELS:(segment + 1) * CHANNELS, :]
+        theirs = sixth(near, far, segment, 1)[:, :128]
+        total += lax.dot_general(mine, theirs, (((1,), (1,)), ((), ())), preferred_element_type=f32)
+    constant[...] = total * (1.0 / math.sqrt(2.0 * SEGMENTS * BINS))
+    loads[3].wait()
 
     def cross(tone):
         return jnp.dot(left_tones[tone].T, right_tones[tone], preferred_element_type=f32)
@@ -350,56 +426,72 @@
         return carry
 
     lax.fori_loop(0, TONES // 4, fold, 0)
+    loads[4].wait()
 
     def lags(pair, carry):
-        rows = pl.ds(pl.multiple_of(pair * 16, 16), 16)
-        base = constant[rows, :]
+        slot = pair % 2
+        base = constant[pl.ds(pl.multiple_of(pair * 16, 16), 16), :]
+
+        @pl.when(pair >= 2)
+        def _():
+            result(pair - 2).wait()
 
         def turn(kind, first, count):
-            both = jnp.dot(lag_table[first * 8:(first + count) * 8, :], folded[kind, pair], preferred_element_type=f32)
+            both = jnp.dot(lag_rows[first * 8:(first + count) * 8, :], folded[kind, pair], preferred_element_type=f32)
             both = both.reshape(count, 8, 256)
             return jnp.concatenate([both[:, :, :128], both[:, :, 128:]], axis=1)
 
         cosines, sines = turn(0, 0, 33) + base, turn(1, 33, 32)
-        out_ref[64, rows, :] = cosines[0].astype(bf16)
+        held[slot, 64, :, :] = cosines[0].astype(bf16)
         for lag in range(1, 33):
             if lag < 32:
-                out_ref[64 + 2 * lag, rows, :] = (cosines[lag] - sines[lag - 1]).astype(bf16)
-            out_ref[64 - 2 * lag, rows, :] = (cosines[lag] + sines[lag - 1]).astype(bf16)
+                held[slot, 64 + 2 * lag, :, :] = (cosines[lag] - sines[lag - 1]).astype(bf16)
+            held[slot, 64 - 2 * lag, :, :] = (cosines[lag] + sines[lag - 1]).astype(bf16)
         cosines, sines = turn(2, 65, 32) + base, turn(3, 97, 32)
         for lag in range(32):
-            out_ref[65 + 2 * lag, rows, :] = (cosines[lag] - sines[lag]).astype(bf16)
-            out_ref[63 - 2 * lag, rows, :] = (cosines[lag] + sines[lag]).astype(bf16)
+            held[slot, 65 + 2 * lag, :, :] = (cosines[lag] - sines[lag]).astype(bf16)
+            held[slot, 63 - 2 * lag, :, :] = (cosines[lag] + sines[lag]).astype(bf16)
+        result(pair).start()
         return carry
 
     lax.fori_loop(0, CHANNELS // 16, lags, 0)
-
-
-def correlate(left_near, left_far, right_near, right_far):
-    tables = [jnp.asarray(table, jnp.bfloat16) for table in (*window_tables(), lag_tables())]
-    vmem = pl.BlockSpec(memory_space=pltpu.VMEM)
+    result(CHANNELS // 16 - 2).wait()
+    result(CHANNELS // 16 - 1).wait()
+
+
+def correlate(left_tones, flat, near, far, right_table, lag_table):
+    hbm = pl.BlockSpec(memory_space=pl.ANY)
     bf16 = jnp.bfloat16
     return pl.pallas_call(
         correlate_kernel,
         out_shape=jax.ShapeDtypeStruct((LAGS, CHANNELS, CHANNELS), bf16),
-        in_specs=[vmem] * 7,
-        out_specs=vmem,
+        in_specs=[hbm] * 6,
+        out_specs=hbm,
         scratch_shapes=[
+            pltpu.VMEM(right_table.shape, bf16),
+            pltpu.VMEM(lag_table.shape, bf16),
+            pltpu.VMEM(left_tones.shape, bf16),
+            pltpu.VMEM(flat.shape, bf16),
+            pltpu.VMEM(near.shape, bf16),
+            pltpu.VMEM(far.shape, bf16),
             pltpu.VMEM((2 * BINS, SEGMENTS * CHANNELS), bf16),
-            pltpu.VMEM((2 * BINS, SEGMENTS * CHANNELS), bf16),
-            pltpu.VMEM((TONES, SEGMENTS * 16, CHANNELS), bf16),
             pltpu.VMEM((TONES, SEGMENTS * 16, 2 * CHANNELS), bf16),
             pltpu.VMEM((4, CHANNELS // 16, TONES // 2 * 8, 256), bf16),
             pltpu.VMEM((CHANNELS, CHANNELS), jnp.float32),
+            pltpu.VMEM((2, LAGS, 16, CHANNELS), bf16),
+            pltpu.SemaphoreType.DMA((5,)),
+            pltpu.SemaphoreType.DMA((PARTS,)),
+            pltpu.SemaphoreType.DMA((2,)),
         ],
         compiler_params=pltpu.CompilerParams(vmem_limit_bytes=56 * 2**20),
-    )(*tables, left_near, left_far, right_near, right_far)
+    )(right_table, lag_table, left_tones, flat, near, far)
 
 
 def per_device(spectra, plan):
-    mine = spectra.reshape(ROWS, BINS)
-    others, near, far = ring_move(plan, mine)
-    return correlate(mine, others, near, far)[None, None]
+    left_table, right_table = (jnp.asarray(table, jnp.bfloat16) for table in window_tables())
+    lag_table = jnp.asarray(lag_tables(), jnp.bfloat16)
+    left_tones, flat, near, far = ring_move(plan, spectra.reshape(ROWS, BINS), left_table)
+    return correlate(left_tones, flat, near, far, right_table, lag_table)[None, None]
 
 
 def solution(mesh):

time: 157 us -> 148 us (0.943)
  Pallas kernels: 150 us -> 146 us
  local copies, waits for them, and re-layouts: 5.24 us -> 1.3 us
    pallas_call x1, Pallas kernels: 27.1 us -> 20.9 us  [correlate(): pl.pallas_call(correlate_kernel, out_shape=jax.ShapeDtypeStruct((LAGS, CH...]
    unnamed x11 -> x1, local copies, waits for them, and re-layouts: 5.24 us -> 1.3 us
    pallas_call x1, Pallas kernels: 123 us -> 125 us  [ring_move(): pl.pallas_call(ring_kernel, out_shape=[jax.ShapeDtypeStruct((TONES, SEGME...]
where the time goes in v4:
time: 148 us; the launch traced here: 147 us
  Pallas kernels  146 us (99%)
    pallas_call x1, Pallas kernels, ring_move(): pl.pallas_call(ring_kernel, out_shape=[jax.ShapeDtypeStruct((TONES, SEGME...  125 us
    pallas_call x1, Pallas kernels, correlate(): pl.pallas_call(correlate_kernel, out_shape=jax.ShapeDtypeStruct((LAGS, CH...  20.9 us

profile of v4, /device:TPU:6, one launch (start us, length us, event | category | flops | bytes accessed | tf_op | source)
XLA Modules:
  0.0 146.9 jit_solution(2018465730344507795)
XLA Ops:
  0.0 1.3 copy.7.plan_ref
  1.3 124.6 %shard_map.64 = (bf16[128,96,128]{2,1,0:T(8,128)(2,1)}, bf16[768,128]{1,0:T(8,128)(2,1)}, bf16[768,512]{1,0:T(8,128)(2,1)}, bf16[768,512]{1,0:T(8,128)(2,1)}) custom-call(s32[2,1]{1,0:T(2,128)} %copy.7.plan_ref, s32[1024]{0:T(1024)} %constant.11.clone.table_ref, bf16[2048,1024]{1,0:T(8,128)(2,1)} %constant.8.clone.left_table, bf16[768,512]{1,0:T(8,128)(2,1)} %bitcast.2), custom_call_target="tpu_custom_call" | custom-call | tf_op jit(solution)/shard_map/pallas_call | solution.py:286
  125.9 20.9 %shard_map.65 = bf16[128,128,128]{2,1,0:T(8,128)(2,1)} custom-call(bf16[2048,1024]{1,0:T(8,128)(2,1)} %constant.9.clone.right_table, bf16[1032,512]{1,0:T(8,128)(2,1)} %constant.10.clone.lag_table, bf16[128,96,128]{2,1,0:T(8,128)(2,1)} %get-tuple-element.9.left_ref, bf16[768,128]{1,0:T(8,128)(2,1)} %get-tuple-element.10.flat_ref, ...), custom_call_target="tpu_custom_call" | custom-call | tf_op jit(solution)/shard_map/pallas_call | solution.py:465

commit v5 on v4

--- a/solution.py
+++ b/solution.py
@@ -13,34 +13,53 @@
 MESH = pl.DeviceIdType.MESH
 RING = 8
 CHUNKS = 4
-SLOTS = 2 * CHUNKS + 2
+SLOTS = 2 * CHUNKS
+WIDTH = 2 * SLOTS + CHUNKS
 STREAMS = 4
 ROWS = 768
 BLOCK = ROWS // CHUNKS
 PIECE = BLOCK // STREAMS
 
 
-def path(mask, place):
-    ahead = ((place ^ mask) - place) % RING
-    first = ((place >> 1) & 1) if mask == 5 else 0
-    return (0, ahead, first) if ahead <= 4 else (1, RING - ahead, first)
-
-
-def ring_table():
-    table = np.zeros((RING, RING, 16), np.int32)
-    for mask in range(RING):
+def ring_plan():
+    sends, lands = {}, {}
+
+    def travel(mask, place, direction, chunk, slots):
+        for hop, slot in enumerate(slots):
+            at = (mask, (place + (hop if direction == 0 else -hop)) % RING, slot, direction)
+            assert at not in sends and slot < SLOTS
+            sends[at] = ("own", chunk) if hop == 0 else ("pass", slots[hop - 1])
+        lands[mask, place ^ mask, chunk] = (direction, slots[-1])
+
+    for mask in range(1, RING):
         for place in range(RING):
-            row = table[mask, place]
-            if mask == 0:
-                row[8:10] = 8
-            elif mask == 4:
-                row[0], row[6], row[8], row[9] = 1, 1, 3, 7
-            else:
-                direction, _, first = path(mask, place)
-                row[direction * 4 + first], row[direction * 4 + first + 2] = 1, 1
-                back, hops, start = path(mask, place ^ mask)
-                row[8:10] = back * 4 + start + hops - 1
-    return table.reshape(-1)
+            ahead = ((place ^ mask) - place) % RING
+            direction, hops = (0, ahead) if ahead <= 4 else (1, RING - ahead)
+            for chunk in range(CHUNKS):
+                if mask == 4:
+                    travel(mask, place, chunk % 2, chunk, [4 * (chunk // 2) + hop for hop in range(4)])
+                elif mask in (3, 7):
+                    slots = [chunk, chunk + 1, chunk + 2] if hops == 3 else [CHUNKS + chunk if chunk else 0]
+                    travel(mask, place, direction, chunk, slots)
+                else:
+                    slots = [[chunk], [chunk, CHUNKS + chunk], [chunk, chunk + 1, CHUNKS + chunk]][hops - 1]
+                    travel(mask, place, direction, chunk, slots)
+
+    sources = [
+        [sorted({what for at, what in sends.items() if at[2:] == (slot, way)}) for way in range(2)] for slot in range(SLOTS)
+    ]
+    spots = [sorted({where for at, where in lands.items() if at[2] == chunk}) + [None] for chunk in range(CHUNKS)]
+    table = np.zeros((RING, RING, WIDTH), np.int32)
+    for (mask, place, slot, way), what in sends.items():
+        table[mask, place, slot * 2 + way] = sources[slot][way].index(what)
+    for chunk in range(CHUNKS):
+        for mask in range(RING):
+            for place in range(RING):
+                table[mask, place, 2 * SLOTS + chunk] = spots[chunk].index(lands.get((mask, place, chunk)))
+    return sources, spots, table.reshape(-1)
+
+
+SOURCES, SPOTS, CODES = ring_plan()
 BINS = 512
 SEGMENTS = 6
 CHANNELS = 128
@@ -48,6 +67,7 @@
 TONES = 128
 SPAN = 2 * TONES
 STEP = 256
+UNROLL = 8
 PARTS = TONES * 16 // STEP
 
 
@@ -81,7 +101,7 @@
         (ch + 1 - ch % 2 * 2, seg),
     ]
     mask = plan_ref[seg, 0] ^ ch
-    bases = [(((mask // 32) % RING) * RING + y) * 16, (((mask // 2) % RING) * RING + z) * 16]
+    bases = [(((mask // 32) % RING) * RING + y) * WIDTH, (((mask // 2) % RING) * RING + z) * WIDTH]
     x_bit, core_bit = mask // 16 % 2, mask % 2
 
     barrier = pltpu.get_barrier_semaphore()
@@ -165,110 +185,119 @@
     forward(0)
     spread(1)
     choose(0)
+    forward(1)
+    spread(2)
     settle(0)
-
+    choose(1)
+    settle(1)
+
+    def beside_slot(stage, slot):
+        if stage == 0:
+            if slot == 0:
+                forward(2)
+                spread(3)
+            elif slot == 1:
+                forward(3)
+                choose(2)
+                settle(2)
+            elif slot == 2:
+                choose(3)
+                settle(3)
+            elif slot == 3:
+                lay_out(mine_ref, opposite, left_turned, range(3))
+            elif slot == 4:
+                lay_out(mine_ref, opposite, left_turned, range(3, 6))
+                flatten()
+            elif slot == 5:
+                load.wait()
+            if slot >= 6:
+                left_part(slot - 6)
+        elif slot < 6:
+            left_part(slot + 2)
+
+    def ring_copy(stage, link, stream, slot):
+        return pltpu.make_async_remote_copy(
+            src_ref=staged.at[link, stream, slot % 2],
+            dst_ref=landed.at[stage, link, stream, slot],
+            send_sem=send_sem.at[link, stream, slot % 2],
+            recv_sem=recv_sem.at[stage, link, stream, slot],
+            device_id=targets[link],
+            device_id_type=MESH,
+        )
+
+    def piece(stream, chunk):
+        return rows(chunk * BLOCK + stream * PIECE, PIECE)
+
+    def each_stream(body):
+        def step(stream, carry):
+            body(stream)
+            return carry
+
+        lax.fori_loop(0, STREAMS, step, 0)
+
+    def send(stage, slot, source):
+        def one(stream):
+            for dim in range(2):
+                for way in range(2):
+                    link = 2 * dim + way
+                    if slot >= 1:
+                        ring_copy(stage, link, stream, slot - 1).wait_recv()
+                    if slot >= 2:
+                        ring_copy(stage, link, stream, slot - 2).wait_send()
+                    code = table_ref[bases[dim] + slot * 2 + way]
+                    value = None
+                    for number, (kind, index) in enumerate(SOURCES[slot][way]):
+                        if kind == "own":
+                            option = source[dim ^ stage][piece(stream, index), :]
+                        else:
+                            option = landed[stage, link, stream, index]
+                        value = option if value is None else jnp.where(code == number, option, value)
+                    staged[link, stream, slot % 2] = value
+                    ring_copy(stage, link, stream, slot).start()
+
+        each_stream(one)
+
+    def pick(stage, chunk, source, goal):
+        def one(stream):
+            for dim in range(2):
+                code = table_ref[bases[dim] + 2 * SLOTS + chunk]
+                value = source[dim ^ stage][piece(stream, chunk), :]
+                for number, spot in enumerate(SPOTS[chunk][:-1]):
+                    value = jnp.where(code == number, landed[stage, 2 * dim + spot[0], stream, spot[1]], value)
+                goal[dim ^ stage][piece(stream, chunk), :] = value
+
+        each_stream(one)
+
+    def drain(stage):
+        def one(stream):
+            for link in range(4):
+                ring_copy(stage, link, stream, SLOTS - 1).wait_recv()
+                ring_copy(stage, link, stream, SLOTS - 2).wait_send()
+                ring_copy(stage, link, stream, SLOTS - 1).wait_send()
+
+        each_stream(one)
+
+    last = [max(spot[1] for spot in spots[:-1]) for spots in SPOTS]
+    sides = [(first.at[0], first.at[1]), (middle.at[0], middle.at[1]), (near_out, far_out)]
+    late = []
     for stage in range(2):
-        source = (first.at[0], first.at[1]) if stage == 0 else (middle.at[0], middle.at[1])
-        goal = (middle.at[0], middle.at[1]) if stage == 0 else (near_out, far_out)
-
-        def piece(stream, chunk):
-            return rows(chunk * BLOCK + stream * PIECE, PIECE)
-
-        def copy(link, stream, slot, stage=stage):
-            return pltpu.make_async_remote_copy(
-                src_ref=staged.at[link, stream, slot % 2],
-                dst_ref=landed.at[stage, link, stream, slot],
-                send_sem=send_sem.at[link, stream, slot % 2],
-                recv_sem=recv_sem.at[stage, link, stream, slot],
-                device_id=targets[link],
-                device_id_type=MESH,
-            )
-
-        def send(slot, first=False, second=False, stage=stage, source=source):
-            for stream in range(STREAMS):
-                for dim in range(2):
-                    chunk = jnp.minimum(slot // 2, CHUNKS - 1)
-                    own = source[dim ^ stage][piece(stream, chunk), :]
-                    for direction in range(2):
-                        link = 2 * dim + direction
-                        value = own
-                        if not first:
-                            copy(link, stream, slot - 1).wait_recv()
-                            if not second:
-                                copy(link, stream, slot - 2).wait_send()
-                            flag = table_ref[bases[dim] + direction * 4 + slot % 4]
-                            value = jnp.where(flag == 1, own, landed[stage, link, stream, slot - 1])
-                        staged[link, stream, slot % 2] = value
-                        copy(link, stream, slot).start()
-
-        def pick(chunk, stage=stage, source=source, goal=goal):
-            for dim in range(2):
-                code = table_ref[bases[dim] + 8 + chunk % 2]
-                for stream in range(STREAMS):
-                    value = source[dim ^ stage][piece(stream, chunk), :]
-                    for place in range(8):
-                        found = landed[stage, 2 * dim + place // 4, stream, 2 * chunk + place % 4]
-                        value = jnp.where(code == place, found, value)
-                    goal[dim ^ stage][piece(stream, chunk), :] = value
-
-        send(0, first=True)
+        source, goal = sides[stage], sides[stage + 1]
+        for slot in range(SLOTS):
+            send(stage, slot, source)
+            for chunk in late:
+                pick(0, chunk, sides[0], sides[1])
+            late = []
+            for chunk in range(CHUNKS):
+                if last[chunk] == slot - 1:
+                    pick(stage, chunk, source, goal)
+            beside_slot(stage, slot)
+        drain(stage)
+        rest = [chunk for chunk in range(CHUNKS) if last[chunk] == SLOTS - 1]
         if stage == 0:
-            forward(1)
-        else:
-            lay_out(mine_ref, opposite, left_turned, range(3))
-        send(1, second=True)
-        if stage == 0:
-            choose(1)
-            spread(2)
-        else:
-            lay_out(mine_ref, opposite, left_turned, range(3, 6))
-            flatten()
-            load.wait()
-
-        def pair(number, carry, stage=stage, send=send, pick=pick):
-            if stage == 0:
-
-                @pl.when(number < CHUNKS)
-                def _():
-                    settle(number)
-
-            send(2 * number)
-            if stage == 0:
-
-                @pl.when(number < CHUNKS - 1)
-                def _():
-                    forward(number + 1)
-
-            else:
-                left_part(2 * number - 2)
-
-            @pl.when(number >= 2)
-            def _():
-                pick(number - 2)
-
-            send(2 * number + 1)
-            if stage == 0:
-
-                @pl.when(number < CHUNKS - 1)
-                def _():
-                    choose(number + 1)
-
-                @pl.when(number < CHUNKS - 2)
-                def _():
-                    spread(number + 2)
-
-            else:
-                left_part(2 * number - 1)
-
-            return carry
-
-        lax.fori_loop(1, SLOTS // 2, pair, 0)
-        for link in range(4):
-            for stream in range(STREAMS):
-                copy(link, stream, SLOTS - 1).wait_recv()
-                copy(link, stream, SLOTS - 2).wait_send()
-                copy(link, stream, SLOTS - 1).wait_send()
-        pick(CHUNKS - 1)
+            late = [chunk for chunk in rest if chunk >= 2]
+        for chunk in rest:
+            if chunk not in late:
+                pick(stage, chunk, source, goal)
 
     for chunk in range(CHUNKS):
         finish(chunk)
@@ -317,7 +346,7 @@
         compiler_params=pltpu.CompilerParams(
             collective_id=0, has_side_effects=True, vmem_limit_bytes=56 * 2**20
         ),
-    )(plan, jnp.asarray(ring_table()), left_table, mine)
+    )(plan, jnp.asarray(CODES), left_table, mine)
 
 
 def window_tables():
@@ -425,7 +454,7 @@
                 folded[kind, group // 2, rows, lanes] = both.astype(bf16)
         return carry
 
-    lax.fori_loop(0, TONES // 4, fold, 0)
+    lax.fori_loop(0, TONES // 4, fold, 0, unroll=UNROLL)
     loads[4].wait()
 
     def lags(pair, carry):

time: 148 us -> 131 us (0.89)
  Pallas kernels: 146 us -> 128 us
    pallas_call x1, Pallas kernels: 125 us -> 112 us  [ring_move(): pl.pallas_call(ring_kernel, out_shape=[jax.ShapeDtypeStruct((TONES, SEGME...]
    pallas_call x1, Pallas kernels: 20.9 us -> 15.7 us  [correlate(): pl.pallas_call(correlate_kernel, out_shape=jax.ShapeDtypeStruct((LAGS, CH...]
where the time goes in v5:
time: 131 us; the launch traced here: 129 us
  Pallas kernels  128 us (98%)
    pallas_call x1, Pallas kernels, ring_move(): pl.pallas_call(ring_kernel, out_shape=[jax.ShapeDtypeStruct((TONES, SEGME...  112 us
    pallas_call x1, Pallas kernels, correlate(): pl.pallas_call(correlate_kernel, out_shape=jax.ShapeDtypeStruct((LAGS, CH...  15.7 us

profile of v5, /device:TPU:6, one launch (start us, length us, event | category | flops | bytes accessed | tf_op | source)
XLA Modules:
  0.0 129.2 jit_solution(18030653333859597331)
XLA Ops:
  0.0 1.3 %copy.7.plan_ref = s32[2,1]{1,0:T(2,128)} copy(s32[2,1]{0,1:T(1,128)} %param.7) | data formatting | bytes 16 | tf_op args[1]
  1.3 112.2 %shard_map.64 = (bf16[128,96,128]{2,1,0:T(8,128)(2,1)}, bf16[768,128]{1,0:T(8,128)(2,1)}, bf16[768,512]{1,0:T(8,128)(2,1)}, bf16[768,512]{1,0:T(8,128)(2,1)}) custom-call(s32[2,1]{1,0:T(2,128)} %copy.7.plan_ref, s32[1280]{0:T(1024)} %constant.11.clone.table_ref, bf16[2048,1024]{1,0:T(8,128)(2,1)} %constant.8.clone.left_table, bf16[768,512]{1,0:T(8,128)(2,1)} %bitcast.2), custom_call_target="tpu_custom_call" | custom-call | tf_op jit(solution)/shard_map/pallas_call | solution.py:315
  113.5 15.7 %shard_map.65 = bf16[128,128,128]{2,1,0:T(8,128)(2,1)} custom-call(bf16[2048,1024]{1,0:T(8,128)(2,1)} %constant.9.clone.right_table, bf16[1032,512]{1,0:T(8,128)(2,1)} %constant.10.clone.lag_table, bf16[128,96,128]{2,1,0:T(8,128)(2,1)} %get-tuple-element.9.left_ref, bf16[768,128]{1,0:T(8,128)(2,1)} %get-tuple-element.10.flat_ref, ...), custom_call_target="tpu_custom_call" | custom-call | tf_op jit(solution)/shard_map/pallas_call | solution.py:494

commit v6 on v5

--- a/solution.py
+++ b/solution.py
@@ -83,11 +83,16 @@
             turned[part * BINS:(part + 1) * BINS, lanes] = sixth(near, far, segment, part).T
 
 
-def ring_kernel(plan_ref, table_ref, left_table, mine_ref, tones_out, flat_out, near_out, far_out, first, middle, beside, across,
+def ring_kernel(plan_in, table_in, left_table, mine_in, tones_out, flat_out, near_out, far_out, first, middle, beside, across,
                 opposite, chosen, swapped, landed, staged, left_rows, left_turned, left_tones, flat, send_sem, recv_sem, x_send,
-                x_recv, load_sem, store_sem):
-    load = pltpu.make_async_copy(left_table, left_rows, load_sem)
-    load.start()
+                x_recv, load_sem, store_sem, plan_ref, table_ref, mine_ref):
+    load = pltpu.make_async_copy(left_table, left_rows, load_sem.at[0])
+    early = [
+        pltpu.make_async_copy(source, goal, load_sem.at[number])
+        for number, (source, goal) in enumerate([(mine_in, mine_ref), (plan_in, plan_ref), (table_in, table_ref)], 1)
+    ]
+    for copy in early:
+        copy.start()
     ch, seg = lax.axis_index("ch"), lax.axis_index("seg")
     z, y = ch // 2 % RING, ch // 32
     turned = ch + 16 - ch // 16 % 2 * 32
@@ -100,10 +105,6 @@
         (turned, 1 - seg),
         (ch + 1 - ch % 2 * 2, seg),
     ]
-    mask = plan_ref[seg, 0] ^ ch
-    bases = [(((mask // 32) % RING) * RING + y) * WIDTH, (((mask // 2) % RING) * RING + z) * WIDTH]
-    x_bit, core_bit = mask // 16 % 2, mask % 2
-
     barrier = pltpu.get_barrier_semaphore()
     for target in targets:
         pl.semaphore_signal(barrier, inc=1, device_id=target, device_id_type=MESH)
@@ -116,8 +117,8 @@
         all_rows = rows(chunk * BLOCK, BLOCK)
         upper, lower = rows(chunk * BLOCK, BLOCK // 2), rows(chunk * BLOCK + BLOCK // 2, BLOCK // 2)
         source, goal, target = [
-            (mine_ref.at[all_rows, :], beside.at[all_rows, :], targets[4]),
-            (mine_ref.at[all_rows, :], across.at[all_rows, :], targets[5]),
+            (mine_in.at[all_rows, :], beside.at[all_rows, :], targets[4]),
+            (mine_in.at[all_rows, :], across.at[all_rows, :], targets[5]),
             (beside.at[upper, :], opposite.at[upper, :], targets[5]),
             (across.at[lower, :], opposite.at[lower, :], targets[4]),
             (chosen.at[0, all_rows, :], swapped.at[0, all_rows, :], targets[6]),
@@ -182,13 +183,19 @@
         pltpu.make_async_copy(flat, flat_out, store_sem.at[PARTS]).start()
 
     spread(0)
+    spread(1)
+    load.start()
+    for copy in early:
+        copy.wait()
+    mask = plan_ref[seg, 0] ^ ch
+    bases = [(((mask // 32) % RING) * RING + y) * WIDTH, (((mask // 2) % RING) * RING + z) * WIDTH]
+    x_bit, core_bit = mask // 16 % 2, mask % 2
     forward(0)
-    spread(1)
+    forward(1)
     choose(0)
-    forward(1)
+    choose(1)
     spread(2)
     settle(0)
-    choose(1)
     settle(1)
 
     def beside_slot(stage, slot):
@@ -197,9 +204,9 @@
                 forward(2)
                 spread(3)
             elif slot == 1:
-                forward(3)
                 choose(2)
                 settle(2)
+                forward(3)
             elif slot == 2:
                 choose(3)
                 settle(3)
@@ -309,7 +316,6 @@
 def ring_move(plan, mine, left_table):
     width = mine.shape[-1]
     vmem = pl.BlockSpec(memory_space=pltpu.VMEM)
-    smem = pl.BlockSpec(memory_space=pltpu.SMEM)
     hbm = pl.BlockSpec(memory_space=pl.ANY)
     bf16 = jnp.bfloat16
     return pl.pallas_call(
@@ -320,7 +326,7 @@
             jax.ShapeDtypeStruct((ROWS, width), bf16),
             jax.ShapeDtypeStruct((ROWS, width), bf16),
         ],
-        in_specs=[smem, smem, hbm, vmem],
+        in_specs=[hbm] * 4,
         out_specs=[hbm, hbm, vmem, vmem],
         scratch_shapes=[
             pltpu.VMEM((2, ROWS, width), bf16),
@@ -340,8 +346,11 @@
             pltpu.SemaphoreType.DMA((2, 4, STREAMS, SLOTS)),
             pltpu.SemaphoreType.DMA((6, CHUNKS)),
             pltpu.SemaphoreType.DMA((6, CHUNKS)),
-            pltpu.SemaphoreType.DMA,
+            pltpu.SemaphoreType.DMA((4,)),
             pltpu.SemaphoreType.DMA((PARTS + 1,)),
+            pltpu.SMEM(plan.shape, jnp.int32),
+            pltpu.SMEM(CODES.shape, jnp.int32),
+            pltpu.VMEM((ROWS, width), bf16),
         ],
         compiler_params=pltpu.CompilerParams(
             collective_id=0, has_side_effects=True, vmem_limit_bytes=56 * 2**20

time: 131 us -> 128 us (0.977)
  Pallas kernels: 128 us -> 125 us
    pallas_call x1, Pallas kernels: 112 us -> 110 us  [ring_move(): pl.pallas_call(ring_kernel, out_shape=[jax.ShapeDtypeStruct((TONES, SEGME...]
where the time goes in v6:
time: 128 us; the launch traced here: 127 us
  Pallas kernels  125 us (98%)
  local copies, waits for them, and re-layouts  1.3 us (1%)
    pallas_call x1, Pallas kernels, ring_move(): pl.pallas_call(ring_kernel, out_shape=[jax.ShapeDtypeStruct((TONES, SEGME...  110 us
    pallas_call x1, Pallas kernels, correlate(): pl.pallas_call(correlate_kernel, out_shape=jax.ShapeDtypeStruct((LAGS, CH...  15.7 us

profile of v6, /device:TPU:6, one launch (start us, length us, event | category | flops | bytes accessed | tf_op | source)
XLA Modules:
  0.0 126.5 jit_solution(11538052907532423402)
XLA Ops:
  0.0 1.3 %copy.7.plan_in = s32[2,1]{1,0:T(2,128)} copy(s32[2,1]{0,1:T(1,128)} %param.7) | data formatting | bytes 16 | tf_op args[1]
  1.3 109.5 %shard_map.64 = (bf16[128,96,128]{2,1,0:T(8,128)(2,1)}, bf16[768,128]{1,0:T(8,128)(2,1)}, bf16[768,512]{1,0:T(8,128)(2,1)}, bf16[768,512]{1,0:T(8,128)(2,1)}) custom-call(s32[2,1]{1,0:T(2,128)} %copy.7.plan_in, s32[1280]{0:T(1024)} %constant.11.clone.table_in, bf16[2048,1024]{1,0:T(8,128)(2,1)} %constant.8.clone.left_table, bf16[768,512]{1,0:T(8,128)(2,1)} %bitcast.2), custom_call_target="tpu_custom_call" | custom-call | tf_op jit(solution)/shard_map/pallas_call | solution.py:321
  110.8 15.7 %shard_map.65 = bf16[128,128,128]{2,1,0:T(8,128)(2,1)} custom-call(bf16[2048,1024]{1,0:T(8,128)(2,1)} %constant.9.clone.right_table, bf16[1032,512]{1,0:T(8,128)(2,1)} %constant.10.clone.lag_table, bf16[128,96,128]{2,1,0:T(8,128)(2,1)} %get-tuple-element.9.left_ref, bf16[768,128]{1,0:T(8,128)(2,1)} %get-tuple-element.10.flat_ref, ...), custom_call_target="tpu_custom_call" | custom-call | tf_op jit(solution)/shard_map/pallas_call | solution.py:503

commit v7 on v6

--- a/solution.py
+++ b/solution.py
@@ -36,14 +36,13 @@
             ahead = ((place ^ mask) - place) % RING
             direction, hops = (0, ahead) if ahead <= 4 else (1, RING - ahead)
             for chunk in range(CHUNKS):
+                go, rest = (0, 1, 3, 5)[chunk], (2, 4, 6, 7)[chunk]
                 if mask == 4:
                     travel(mask, place, chunk % 2, chunk, [4 * (chunk // 2) + hop for hop in range(4)])
                 elif mask in (3, 7):
-                    slots = [chunk, chunk + 1, chunk + 2] if hops == 3 else [CHUNKS + chunk if chunk else 0]
-                    travel(mask, place, direction, chunk, slots)
+                    travel(mask, place, direction, chunk, [go, go + 1, go + 2] if hops == 3 else [(0, 3, 5, 7)[chunk]])
                 else:
-                    slots = [[chunk], [chunk, CHUNKS + chunk], [chunk, chunk + 1, CHUNKS + chunk]][hops - 1]
-                    travel(mask, place, direction, chunk, slots)
+                    travel(mask, place, direction, chunk, [[go], [go, rest], [go, go + 1, rest]][hops - 1])
 
     sources = [
         [sorted({what for at, what in sends.items() if at[2:] == (slot, way)}) for way in range(2)] for slot in range(SLOTS)
@@ -187,7 +186,7 @@
     load.start()
     for copy in early:
         copy.wait()
-    mask = plan_ref[seg, 0] ^ ch
+    mask = plan_ref[0, seg] ^ ch
     bases = [(((mask // 32) % RING) * RING + y) * WIDTH, (((mask // 2) % RING) * RING + z) * WIDTH]
     x_bit, core_bit = mask // 16 % 2, mask % 2
     forward(0)
@@ -205,12 +204,12 @@
                 spread(3)
             elif slot == 1:
                 choose(2)
-                settle(2)
                 forward(3)
             elif slot == 2:
+                settle(2)
                 choose(3)
+            elif slot == 3:
                 settle(3)
-            elif slot == 3:
                 lay_out(mine_ref, opposite, left_turned, range(3))
             elif slot == 4:
                 lay_out(mine_ref, opposite, left_turned, range(3, 6))
@@ -348,14 +347,14 @@
             pltpu.SemaphoreType.DMA((6, CHUNKS)),
             pltpu.SemaphoreType.DMA((4,)),
             pltpu.SemaphoreType.DMA((PARTS + 1,)),
-            pltpu.SMEM(plan.shape, jnp.int32),
+            pltpu.SMEM((1, plan.shape[0]), jnp.int32),
             pltpu.SMEM(CODES.shape, jnp.int32),
             pltpu.VMEM((ROWS, width), bf16),
         ],
         compiler_params=pltpu.CompilerParams(
             collective_id=0, has_side_effects=True, vmem_limit_bytes=56 * 2**20
         ),
-    )(plan, jnp.asarray(CODES), left_table, mine)
+    )(plan.T, jnp.asarray(CODES), left_table, mine)
 
 
 def window_tables():
@@ -410,14 +409,16 @@
 
     for load in loads[:2]:
         load.start()
-    for number in range(PARTS):
+    for number in range(2):
+        part_load(number).start()
+
+    loads[0].wait()
+    lay_out(near, far, right_turned, range(3))
+    loads[1].wait()
+    for number in range(2, PARTS):
         part_load(number).start()
     for load in loads[2:]:
         load.start()
-
-    loads[0].wait()
-    lay_out(near, far, right_turned, range(3))
-    loads[1].wait()
     lay_out(near, far, right_turned, range(3, 6))
 
     def tones_of(number, carry):

time: 128 us -> 125 us (0.977)
  local copies, waits for them, and re-layouts: 1.3 us -> 0 us
    unnamed x1 -> x0, local copies, waits for them, and re-layouts: 1.3 us -> none
where the time goes in v7:
time: 125 us
  Pallas kernels  125 us (100%)
    pallas_call x1, Pallas kernels, ring_move(): pl.pallas_call(ring_kernel, out_shape=[jax.ShapeDtypeStruct((TONES, SEGME...  109 us
    pallas_call x1, Pallas kernels, correlate(): pl.pallas_call(correlate_kernel, out_shape=jax.ShapeDtypeStruct((LAGS, CH...  15.2 us

profile of v7, /device:TPU:6, one launch (start us, length us, event | category | flops | bytes accessed | tf_op | source)
XLA Modules:
  0.0 124.7 jit_solution(7692111435078263718)
XLA Ops:
  0.0 109.5 %shard_map.64 = (bf16[128,96,128]{2,1,0:T(8,128)(2,1)}, bf16[768,128]{1,0:T(8,128)(2,1)}, bf16[768,512]{1,0:T(8,128)(2,1)}, bf16[768,512]{1,0:T(8,128)(2,1)}) custom-call(s32[1,2]{1,0:T(1,128)} %bitcast.4, s32[1280]{0:T(1024)} %constant.11.clone.table_in, bf16[2048,1024]{1,0:T(8,128)(2,1)} %constant.8.clone.left_table, bf16[768,512]{1,0:T(8,128)(2,1)} %bitcast.3), custom_call_target="tpu_custom_call" | custom-call | tf_op jit(solution)/shard_map/pallas_call | solution.py:320
  109.5 15.2 %shard_map.65 = bf16[128,128,128]{2,1,0:T(8,128)(2,1)} custom-call(bf16[2048,1024]{1,0:T(8,128)(2,1)} %constant.9.clone.right_table, bf16[1032,512]{1,0:T(8,128)(2,1)} %constant.10.clone.lag_table, bf16[128,96,128]{2,1,0:T(8,128)(2,1)} %get-tuple-element.9.left_ref, bf16[768,128]{1,0:T(8,128)(2,1)} %get-tuple-element.10.flat_ref, ...), custom_call_target="tpu_custom_call" | custom-call | tf_op jit(solution)/shard_map/pallas_call | solution.py:504

commit v8 on v7

--- a/solution.py
+++ b/solution.py
@@ -66,7 +66,7 @@
 TONES = 128
 SPAN = 2 * TONES
 STEP = 256
-UNROLL = 8
+UNROLL = 16
 PARTS = TONES * 16 // STEP
 
 
@@ -191,17 +191,17 @@
     x_bit, core_bit = mask // 16 % 2, mask % 2
     forward(0)
     forward(1)
+    spread(2)
     choose(0)
+    settle(0)
     choose(1)
-    spread(2)
-    settle(0)
+    spread(3)
     settle(1)
 
     def beside_slot(stage, slot):
         if stage == 0:
             if slot == 0:
                 forward(2)
-                spread(3)
             elif slot == 1:
                 choose(2)
                 forward(3)

time: 125 us -> 122 us (0.976)
  Pallas kernels: 125 us -> 121 us
    pallas_call x1, Pallas kernels: 109 us -> 106 us  [ring_move(): pl.pallas_call(ring_kernel, out_shape=[jax.ShapeDtypeStruct((TONES, SEGME...]
where the time goes in v8:
time: 122 us; the launch traced here: 121 us
  Pallas kernels  121 us (99%)
    pallas_call x1, Pallas kernels, ring_move(): pl.pallas_call(ring_kernel, out_shape=[jax.ShapeDtypeStruct((TONES, SEGME...  106 us
    pallas_call x1, Pallas kernels, correlate(): pl.pallas_call(correlate_kernel, out_shape=jax.ShapeDtypeStruct((LAGS, CH...  14.8 us

profile of v8, /device:TPU:6, one launch (start us, length us, event | category | flops | bytes accessed | tf_op | source)
XLA Modules:
  0.0 121.2 jit_solution(15006498689440253147)
XLA Ops:
  0.0 106.4 %shard_map.64 = (bf16[128,96,128]{2,1,0:T(8,128)(2,1)}, bf16[768,128]{1,0:T(8,128)(2,1)}, bf16[768,512]{1,0:T(8,128)(2,1)}, bf16[768,512]{1,0:T(8,128)(2,1)}) custom-call(s32[1,2]{1,0:T(1,128)} %bitcast.4, s32[1280]{0:T(1024)} %constant.11.clone.table_in, bf16[2048,1024]{1,0:T(8,128)(2,1)} %constant.8.clone.left_table, bf16[768,512]{1,0:T(8,128)(2,1)} %bitcast.3), custom_call_target="tpu_custom_call" | custom-call | tf_op jit(solution)/shard_map/pallas_call | solution.py:320
  106.4 14.8 %shard_map.65 = bf16[128,128,128]{2,1,0:T(8,128)(2,1)} custom-call(bf16[2048,1024]{1,0:T(8,128)(2,1)} %constant.9.clone.right_table, bf16[1032,512]{1,0:T(8,128)(2,1)} %constant.10.clone.lag_table, bf16[128,96,128]{2,1,0:T(8,128)(2,1)} %get-tuple-element.9.left_ref, bf16[768,128]{1,0:T(8,128)(2,1)} %get-tuple-element.10.flat_ref, ...), custom_call_target="tpu_custom_call" | custom-call | tf_op jit(solution)/shard_map/pallas_call | solution.py:504

commit v9 on v8

--- a/solution.py
+++ b/solution.py
@@ -84,7 +84,7 @@
 
 def ring_kernel(plan_in, table_in, left_table, mine_in, tones_out, flat_out, near_out, far_out, first, middle, beside, across,
                 opposite, chosen, swapped, landed, staged, left_rows, left_turned, left_tones, flat, send_sem, recv_sem, x_send,
-                x_recv, load_sem, store_sem, plan_ref, table_ref, mine_ref):
+                x_recv, load_sem, store_sem, plan_ref, table_ref, mine_ref, last_half, out_sem):
     load = pltpu.make_async_copy(left_table, left_rows, load_sem.at[0])
     early = [
         pltpu.make_async_copy(source, goal, load_sem.at[number])
@@ -273,6 +273,16 @@
                 goal[dim ^ stage][piece(stream, chunk), :] = value
 
         each_stream(one)
+        if stage == 1:
+            for copy in give(chunk):
+                copy.start()
+
+    def give(chunk):
+        here = rows(chunk * BLOCK, BLOCK)
+        return [
+            pltpu.make_async_copy(last_half.at[half, here, :], goal.at[here, :], out_sem.at[half, chunk])
+            for half, goal in enumerate((near_out, far_out))
+        ]
 
     def drain(stage):
         def one(stream):
@@ -284,7 +294,7 @@
         each_stream(one)
 
     last = [max(spot[1] for spot in spots[:-1]) for spots in SPOTS]
-    sides = [(first.at[0], first.at[1]), (middle.at[0], middle.at[1]), (near_out, far_out)]
+    sides = [(first.at[0], first.at[1]), (middle.at[0], middle.at[1]), (last_half.at[0], last_half.at[1])]
     late = []
     for stage in range(2):
         source, goal = sides[stage], sides[stage + 1]
@@ -309,12 +319,14 @@
         finish(chunk)
     for number in range(PARTS):
         store(number).wait()
+    for chunk in range(CHUNKS):
+        for copy in give(chunk):
+            copy.wait()
     pltpu.make_async_copy(flat, flat_out, store_sem.at[PARTS]).wait()
 
 
 def ring_move(plan, mine, left_table):
     width = mine.shape[-1]
-    vmem = pl.BlockSpec(memory_space=pltpu.VMEM)
     hbm = pl.BlockSpec(memory_space=pl.ANY)
     bf16 = jnp.bfloat16
     return pl.pallas_call(
@@ -326,7 +338,7 @@
             jax.ShapeDtypeStruct((ROWS, width), bf16),
         ],
         in_specs=[hbm] * 4,
-        out_specs=[hbm, hbm, vmem, vmem],
+        out_specs=[hbm] * 4,
         scratch_shapes=[
             pltpu.VMEM((2, ROWS, width), bf16),
             pltpu.VMEM((2, ROWS, width), bf16),
@@ -350,6 +362,8 @@
             pltpu.SMEM((1, plan.shape[0]), jnp.int32),
             pltpu.SMEM(CODES.shape, jnp.int32),
             pltpu.VMEM((ROWS, width), bf16),
+            pltpu.VMEM((2, ROWS, width), bf16),
+            pltpu.SemaphoreType.DMA((2, CHUNKS)),
         ],
         compiler_params=pltpu.CompilerParams(
             collective_id=0, has_side_effects=True, vmem_limit_bytes=56 * 2**20

time: 122 us -> 122 us (level)
  no operation moved by 1% of the time
where the time goes in v9:
time: 122 us; the launch traced here: 121 us
  Pallas kernels  121 us (99%)
    pallas_call x1, Pallas kernels, ring_move(): pl.pallas_call(ring_kernel, out_shape=[jax.ShapeDtypeStruct((TONES, SEGME...  106 us
    pallas_call x1, Pallas kernels, correlate(): pl.pallas_call(correlate_kernel, out_shape=jax.ShapeDtypeStruct((LAGS, CH...  14.8 us

profile of v9, /device:TPU:6, one launch (start us, length us, event | category | flops | bytes accessed | tf_op | source)
XLA Modules:
  0.0 120.9 jit_solution(7661961136282033358)
XLA Ops:
  0.0 106.0 %shard_map.64 = (bf16[128,96,128]{2,1,0:T(8,128)(2,1)}, bf16[768,128]{1,0:T(8,128)(2,1)}, bf16[768,512]{1,0:T(8,128)(2,1)}, bf16[768,512]{1,0:T(8,128)(2,1)}) custom-call(s32[1,2]{1,0:T(1,128)} %bitcast.4, s32[1280]{0:T(1024)} %constant.11.clone.table_in, bf16[2048,1024]{1,0:T(8,128)(2,1)} %constant.8.clone.left_table, bf16[768,512]{1,0:T(8,128)(2,1)} %bitcast.3), custom_call_target="tpu_custom_call" | custom-call | tf_op jit(solution)/shard_map/pallas_call | solution.py:332
  106.0 14.8 %shard_map.65 = bf16[128,128,128]{2,1,0:T(8,128)(2,1)} custom-call(bf16[2048,1024]{1,0:T(8,128)(2,1)} %constant.9.clone.right_table, bf16[1032,512]{1,0:T(8,128)(2,1)} %constant.10.clone.lag_table, bf16[128,96,128]{2,1,0:T(8,128)(2,1)} %get-tuple-element.9.left_ref, bf16[768,128]{1,0:T(8,128)(2,1)} %get-tuple-element.10.flat_ref, ...), custom_call_target="tpu_custom_call" | custom-call | tf_op jit(solution)/shard_map/pallas_call | solution.py:518
